TPU v7x, 32 devices: a whole 2x2x4 slice. The times are simulated.
32 devices in a mesh: shot: 4 (over x, core), gx: 4 (over z), gy: 2 (over y).
Axes of the slice: x: 2, y: 2, z: 4, core: 2. Of those that a mesh axis runs over, the one named last changes fastest.
Arguments:
- velocity: bfloat16 [512, 64, 256], P(('shot', 'gx'), 'gy'), may hold values from 0.14941406 to 0.34960938
- epsilon: bfloat16 [512, 64, 256], P(('shot', 'gx'), 'gy'), may hold values from 0.049804688 to 0.29882812
- delta: bfloat16 [512, 64, 256], P(('shot', 'gx'), 'gy'), may hold values from 0.019897461 to 0.14941406
- anchors: int32 [4], replicated, may hold values from 0 to 384
- sources: int32 [4, 3], P('shot'), may hold values from 0 to 255, as said below
- wavelet: float32 [4, 4], P('shot'), may hold values from -8 to 8
- p_now: float32 [4, 128, 64, 256], P('shot', 'gx', 'gy'), may hold values from -6 to 6
- p_prev: float32 [4, 128, 64, 256], P('shot', 'gx', 'gy'), may hold values from -6 to 6
- q_now: float32 [4, 128, 64, 256], P('shot', 'gx', 'gy'), may hold values from -6 to 6
- q_prev: float32 [4, 128, 64, 256], P('shot', 'gx', 'gy'), may hold values from -6 to 6
Outputs:
- p_out: float32 [4, 128, 64, 256], P('shot', 'gx', 'gy')
- q_out: float32 [4, 128, 64, 256], P('shot', 'gx', 'gy')
Inputs may be any that keep to these rules, and one draw needn't show every extreme that they name: `sources`: each source lies inside its aperture: x below 128, y below 64, z below 256; some source lies on the aperture's far end along its longest dimension, and some source has x equal to 0.
All inputs are finite; a program needn't handle non-finite values.
Results may differ from a plain program's by a relative error of at most 0.0003.
Values may be sent and summed in bfloat16 or wider, within the bound.
No kernel may reach another device: no remote copies, remote signals or barrier semaphores. Data moves between devices by JAX's collectives and lax.ppermute only.
A program may use at most 128 MiB of HBM per device.

v0:
```python
import functools

import jax
import jax.numpy as jnp
import numpy as np
from jax import lax
from jax.experimental import pallas as pl
from jax.experimental.pallas import tpu as pltpu
from jax.sharding import PartitionSpec as P

STEPS = 4
REACH = 4
SCALE = 5040.0
CENTER = -14350.0
OUTER = (8064.0, -1008.0, 128.0, -9.0)
BUCKET = 4
XT = 8
VMEM_LIMIT = 16 * 1024 * 1024


def row_group(anchor, gx, n_gx, rows):
    period = n_gx * rows
    group = lax.div(anchor, period)
    cut = lax.rem(anchor, period) - gx * rows
    return lambda i: jnp.where(i < cut, group + 1, group)


def pick_kernel(n_gx, ids_ref, anchors_ref, field_ref, other_ref, send_ref, here_ref):
    rows = field_ref.shape[0]
    shot, gx = ids_ref[0], ids_ref[1]
    core = shot & 1
    far = row_group(anchors_ref[shot ^ 2], gx, n_gx, rows)
    own = row_group(anchors_ref[shot], gx, n_gx, rows)
    for i in range(rows):
        field, other = field_ref[i], other_ref[i]
        send_ref[i] = jnp.where(far(i) & 1 == core, field, other)
        here_ref[i] = jnp.where(own(i) & 1 == core, field, other)


def join_kernel(n_gx, whose, ids_ref, anchors_ref, *refs):
    *blocks, out_ref = refs
    rows = out_ref.shape[0]
    shot, gx = ids_ref[0], ids_ref[1]
    core, half = shot & 1, shot >> 1
    own = row_group(anchors_ref[shot ^ whose], gx, n_gx, rows)
    for i in range(rows):
        here, across = blocks[0][i], blocks[1][i]
        if len(blocks) == 4:
            mine = own(i) & 1 == core
            here, across = jnp.where(mine, here, blocks[2][i]), jnp.where(mine, across, blocks[3][i])
        out_ref[i] = jnp.where(own(i) >> 1 == half, here, across)


def facts_kernel(n_gx, shape, ids_ref, anchors_ref, sources_ref, wavelet_ref, facts_ref, waves_ref, *index_refs):
    nx, ny, nz = shape
    gx, gy = ids_ref[1], ids_ref[2]
    for k, index_ref in enumerate(index_refs):
        anchor = anchors_ref[ids_ref[0] ^ (2 * k)]
        turn = lax.rem(lax.div(anchor, nx), n_gx)
        rest = lax.rem(anchor, nx)
        bucket = jnp.where(rest > 0, lax.div(rest - 1, BUCKET) + 1, 0)
        index_ref[0] = turn * (nx // BUCKET + 1) + bucket
    lx, ly = sources_ref[0, 0] - gx * nx, sources_ref[0, 1] - gy * ny
    cell = jnp.where((lx >= 0) & (lx < nx) & (ly >= 0) & (ly < ny), lx * ny + ly, -1)
    for k, fact in enumerate((gx & 1, gy & 1, cell, sources_ref[0, 2])):
        facts_ref[k : k + 1] = jnp.full((1, nz), fact, jnp.int32)
    for k in range(STEPS):
        waves_ref[k : k + 1] = jnp.full((1, nz), wavelet_ref[0, k], jnp.float32)


def rotation_branches(n_gx, rows):
    def perm(block, by):
        by %= n_gx
        if by == 0:
            return block
        return lax.ppermute(block, "gx", [(i, (i - by) % n_gx) for i in range(n_gx)])

    def branch(turn, bucket):
        def aligned(block):
            moved = perm(block, turn)
            return jnp.concatenate([moved, jnp.zeros_like(moved[: BUCKET - 1])], 0)

        def split(block):
            k = BUCKET * (bucket - 1)
            return jnp.concatenate(
                [perm(block[k + 1 :], turn), perm(block[: k + BUCKET], turn + 1)], 0
            )

        return aligned if bucket == 0 else split

    return [branch(t, b) for t in range(n_gx) for b in range(rows // BUCKET + 1)]


def model_windows(ids, anchors, fields, index, rims):
    n_gx = lax.axis_size("gx")
    n_shot = lax.axis_size("shot")
    branches = rotation_branches(n_gx, fields[0].shape[0])
    beside = [(i, i ^ 1) for i in range(n_shot)]
    across = [(i, i ^ 2) for i in range(n_shot)]
    like = jax.ShapeDtypeStruct(fields[0].shape, fields[0].dtype)

    def turned(k, whose, *blocks):
        (block,) = call(
            functools.partial(join_kernel, n_gx, whose), f"join_{k}", [ids, anchors], in_vmem(*blocks), [like]
        )
        return lax.switch(index[whose // 2][0], branches, block)

    crossed = [lax.ppermute(fields[0], "shot", across)]
    others = [lax.ppermute(field, "shot", beside) for field in fields]
    sends, heres = [None], [None]
    for k in (1, 2):
        send, here = call(
            functools.partial(pick_kernel, n_gx), f"pick_{k}", [ids, anchors], in_vmem(fields[k], others[k]), [like] * 2
        )
        sends.append(send)
        heres.append(here)
    sends[1], sends[2], crossed[0], rims, index = lax.optimization_barrier((sends[1], sends[2], crossed[0], rims, index))
    crossed += [lax.ppermute(send, "shot", across) for send in sends[1:]]
    far_other = lax.ppermute(crossed[0], "shot", beside)
    windows = [turned(0, 2, fields[0], crossed[0], others[0], far_other)]
    crossed[1], windows[0] = lax.optimization_barrier((crossed[1], windows[0]))
    windows.append(turned(1, 0, heres[1], crossed[1]))
    crossed[2], windows[0], windows[1] = lax.optimization_barrier((crossed[2], windows[0], windows[1]))
    windows[0] = lax.ppermute(windows[0], "shot", across)
    windows.append(turned(2, 0, heres[2], crossed[2]))
    return windows, rims


def swaps(count):
    near = [(i, i ^ 1) for i in range(count)]
    off = [(i, i + 1) for i in range(1, count - 1, 2)]
    return [near] + [off + [(b, a) for a, b in off]] * bool(off)


def exchange(rims):
    sets = [("gx", pairs) for pairs in swaps(lax.axis_size("gx"))] + [("gy", pairs) for pairs in swaps(lax.axis_size("gy"))]
    return [lax.ppermute(rim, axis, pairs) for rim, (axis, pairs) in zip(rims, sets, strict=True)]


def depth_matrix(nz):
    out = np.zeros((nz, nz), np.float32)
    for k, weight in enumerate(OUTER, 1):
        out += weight * (np.eye(nz, k=k, dtype=np.float32) + np.eye(nz, k=-k, dtype=np.float32))
    return out


def plane_matrix(ny):
    out = np.zeros((XT, ny, XT + 2 * REACH, ny), np.float32)
    column = depth_matrix(ny)
    for x in range(XT):
        out[x, :, x + REACH, :] = column
        for k, weight in enumerate(OUTER, 1):
            for at in (x + REACH - k, x + REACH + k):
                out[x, np.arange(ny), at, np.arange(ny)] += weight
    return out.reshape(XT * ny, (XT + 2 * REACH) * ny)


def side_matrix(nx):
    out = np.zeros((nx, 16, 2, REACH + 1, nx), np.float32)
    x = np.arange(nx)
    for cell in range(REACH):
        for plane in range(REACH + 1):
            reach = cell + plane % REACH
            if reach < REACH:
                out[x, cell, 0, plane, x] = OUTER[reach]
                out[x, 15 - cell, 1, plane, x] = OUTER[reach]
    return out.reshape(nx * 16, 2 * (REACH + 1) * nx)


def split(values):
    high = values.astype(jnp.bfloat16)
    return high, (values - high.astype(jnp.float32)).astype(jnp.bfloat16)


def dot(a, b):
    return jnp.dot(a, b, preferred_element_type=jnp.float32)


def neighbours(p_ref, q_ref, dh_ref, dz_ref, high_ref, low_ref, use, before=None):
    nx, ny, nz = p_ref.shape
    flat = (XT * ny, nz)
    for ref in (high_ref, low_ref):
        ref[0:REACH] = jnp.zeros((REACH, ny, nz), jnp.bfloat16)
        ref[nx + REACH :] = jnp.zeros((REACH, ny, nz), jnp.bfloat16)

    def cut(i, _):
        x = i * XT
        high, low = split(p_ref[pl.ds(x, XT)])
        high_ref[pl.ds(x + REACH, XT)] = high
        low_ref[pl.ds(x + REACH, XT)] = low
        return _

    lax.fori_loop(0, nx // XT, cut, None)

    def tile(i, _):
        if before:
            before(i)
        x = i * XT
        rows = pl.ds(x, XT)
        p, q = p_ref[rows].reshape(flat), q_ref[rows].reshape(flat)
        window = pl.ds(x, XT + 2 * REACH)
        deep = ((XT + 2 * REACH) * ny, nz)
        both = jnp.concatenate([high_ref[window].reshape(deep), low_ref[window].reshape(deep)], 0)
        across = dot(jnp.concatenate([dh_ref[...]] * 2, 1), both)
        down = dot(jnp.concatenate(split(q), 1), jnp.concatenate([dz_ref[...]] * 2, 0))
        use(i, rows, p, q, across + (2 * CENTER) * p, down + CENTER * q)
        return _

    lax.fori_loop(0, nx // XT, tile, None)


def rim_terms(facts_ref, rim_refs, ds_ref, shape):
    nx, ny, nz = shape
    xa_ref, xb_ref, ya_ref, *yb_ref = rim_refs
    x_odd = jnp.broadcast_to(facts_ref[0:1], (ny, nz)) == 1
    below, above = [], []
    for d in range(REACH):
        xa, xb = (ref[d * ny : (d + 1) * ny].astype(jnp.float32) for ref in (xa_ref, xb_ref))
        if d == 0:
            xa, xb = (v + ref[REACH * ny :].astype(jnp.float32) for v, ref in ((xa, xa_ref), (xb, xb_ref)))
        below.append(jnp.where(x_odd, xa, xb))
        above.append(jnp.where(x_odd, xb, xa))
    near, far = [], []
    for i in range(REACH):
        near.append(sum(OUTER[i + d] * below[d] for d in range(REACH - i)))
        far.insert(0, sum(OUTER[i + d] * above[d] for d in range(REACH - i)))
    ya = ya_ref[...]
    y_odd = jnp.broadcast_to(facts_ref[1:2].astype(jnp.float32).astype(ya.dtype), ya.shape)
    low_side, high_side = ya * y_odd, ya * (1 - y_odd)
    if yb_ref:
        yb = yb_ref[0][...]
        low_side, high_side = low_side + yb * (1 - y_odd), high_side + yb * y_odd
    side = dot(ds_ref[...], jnp.concatenate([low_side, high_side], 0))
    return jnp.stack(near), jnp.stack(far), side.reshape(nx, 16, nz)


def put_rims(facts_ref, low_ref, high_ref, head_ref, tail_ref, sxa_ref, sxb_ref, sya_ref, *syb_ref):
    _, ny, nz = low_ref.shape
    nx, cells, _ = head_ref.shape
    x_odd = jnp.broadcast_to(facts_ref[0:1], (ny, nz)) == 1
    y_odd = jnp.broadcast_to(facts_ref[1:2], (nx, nz)) == 1
    for d in range(REACH):
        low, high = low_ref[d], high_ref[REACH - 1 - d]
        put_plane(d, sxa_ref, jnp.where(x_odd, low, high))
        put_plane(d, sxb_ref, jnp.where(x_odd, high, low))
        head, tail = head_ref[:, d, :], tail_ref[:, cells - 1 - d, :]
        put_plane(d, sya_ref, jnp.where(y_odd, head, tail))
        if syb_ref:
            put_plane(d, syb_ref[0], jnp.where(y_odd, tail, head))


def put_plane(d, ref, plane):
    high, low = split(plane)
    count = plane.shape[0]
    ref[d * count : (d + 1) * count] = high
    if d == 0:
        ref[REACH * count :] = low


def put_rims_of(facts_ref, p_ref, *rim_refs):
    nx, ny, _ = p_ref.shape
    low, high = p_ref.at[0:REACH], p_ref.at[nx - REACH : nx]
    put_rims(facts_ref, low, high, p_ref, p_ref, *rim_refs)


def edge_kernel(facts_ref, p_hbm, *refs):
    *rim_refs, low_ref, high_ref, head_ref, tail_ref, sem = refs
    nx, ny, _ = p_hbm.shape
    parts = (p_hbm.at[0:REACH], p_hbm.at[nx - REACH : nx], p_hbm.at[:, 0:8], p_hbm.at[:, ny - 8 : ny])
    held = (low_ref, high_ref, head_ref, tail_ref)
    copies = [pltpu.make_async_copy(src, dst, sem.at[k]) for k, (src, dst) in enumerate(zip(parts, held))]
    for copy in copies:
        copy.start()
    for copy in copies:
        copy.wait()
    put_rims(facts_ref, *held, *rim_refs)


def add_rims(terms, p_in, q_in, a_ref, b_ref, p_ref, q_ref):
    near, far, side = terms
    nx, ny, nz = p_ref.shape
    for rows, term in ((slice(0, REACH), near), (slice(nx - REACH, nx), far)):
        p_ref[rows] = p_in[rows] + a_ref[rows] * term
        q_ref[rows] = q_in[rows] + b_ref[rows] * term
    for cells, term in ((slice(0, 8), side[:, 0:8]), (slice(ny - 8, ny), side[:, 8:16])):
        p_ref[:, cells] += a_ref[:, cells] * term
        q_ref[:, cells] += b_ref[:, cells] * term


def first_kernel(n_rims, ids_ref, anchors_ref, facts_ref, wave_ref, p0_ref, q0_ref, dh_ref, dz_ref, ds_ref, *refs):
    sources, rims_hbm, refs = refs[:5], refs[5 : 5 + n_rims], refs[5 + n_rims :]
    p_ref, q_ref, a_ref, b_ref, c_ref = refs[:5]
    send_refs, refs = refs[5 : 5 + n_rims], refs[5 + n_rims :]
    high_ref, low_ref, pb_ref, qb_ref, v_ref, e_ref, d_ref = refs[:7]
    held, rim_refs, (sem, rim_sem) = refs[2:7], refs[7 : 7 + n_rims], refs[7 + n_rims :]
    nx, ny, nz = p_ref.shape
    f32 = jnp.float32

    def loads(i):
        out = []
        for k, (src, dst) in enumerate(zip(sources, held)):
            start = i * XT + (first if k >= 2 else 0)
            out.append(pltpu.make_async_copy(src.at[pl.ds(start, XT)], dst.at[pl.ds(i * XT, XT)], sem.at[k, i]))
        return out

    rest = lax.rem(anchors_ref[ids_ref[0]], nx)
    first = jnp.where(rest > 0, lax.rem(rest - 1, BUCKET), 0)
    for i in range(nx // XT):
        for load in loads(i):
            load.start()
    rim_loads = [pltpu.make_async_copy(src, dst, rim_sem.at[k]) for k, (src, dst) in enumerate(zip(rims_hbm, rim_refs))]
    for load in rim_loads:
        load.start()

    def arrive(i):
        for load in loads(i):
            load.wait()

    def use(i, rows, p, q, across, down):
        flat = p.shape
        c = v_ref[rows].reshape(flat).astype(f32)
        c = c * c * f32(1.0 / SCALE)
        a = c * (1.0 + 2.0 * e_ref[rows].reshape(flat).astype(f32))
        b = c * jnp.sqrt(1.0 + 2.0 * d_ref[rows].reshape(flat).astype(f32))
        for ref, value in ((a_ref, a), (b_ref, b), (c_ref, c)):
            ref[rows] = value.reshape((XT, ny, nz))
        update(0, i, rows, p, q, across, down, facts_ref, wave_ref, pb_ref, qb_ref, a, b, c, p_ref, q_ref)

    neighbours(p0_ref, q0_ref, dh_ref, dz_ref, high_ref, low_ref, use, arrive)
    for load in rim_loads:
        load.wait()
    terms = rim_terms(facts_ref, rim_refs, ds_ref, p_ref.shape)
    add_rims(terms, p_ref, q_ref, a_ref, b_ref, p_ref, q_ref)
    put_rims_of(facts_ref, p_ref, *send_refs)


def update(step, i, rows, p, q, across, down, facts_ref, wave_ref, pb_ref, qb_ref, a, b, c, po_ref, qo_ref):
    flat = p.shape
    pb, qb = pb_ref[rows].reshape(flat), qb_ref[rows].reshape(flat)
    block = (XT,) + po_ref.shape[1:]
    at_row = lax.broadcasted_iota(jnp.int32, flat, 0) == jnp.broadcast_to(facts_ref[2:3] - i * flat[0], flat)
    at_z = lax.broadcasted_iota(jnp.int32, flat, 1) == jnp.broadcast_to(facts_ref[3:4], flat)
    source = jnp.where(at_row & at_z, jnp.broadcast_to(wave_ref[step : step + 1], flat), 0.0)
    po_ref[rows] = (2.0 * p - pb + (a * across + b * down) + source).reshape(block)
    qo_ref[rows] = (2.0 * q - qb + (b * across + c * down)).reshape(block)


def inner_kernel(step, facts_ref, wave_ref, p_ref, pb_ref, q_ref, qb_ref, a_ref, b_ref, c_ref, dh_ref, dz_ref,
                 po_ref, qo_ref, high_ref, low_ref):
    def use(i, rows, p, q, across, down):
        a, b, c = (ref[rows].reshape(p.shape) for ref in (a_ref, b_ref, c_ref))
        update(step, i, rows, p, q, across, down, facts_ref, wave_ref, pb_ref, qb_ref, a, b, c, po_ref, qo_ref)

    neighbours(p_ref, q_ref, dh_ref, dz_ref, high_ref, low_ref, use)


def rim_kernel(n_rims, last, facts_ref, p_in, q_in, a_ref, b_ref, *refs):
    rim_refs, (ds_ref, p_ref, q_ref, *out_refs) = refs[:n_rims], refs[n_rims:]
    near, far, side = rim_terms(facts_ref, rim_refs, ds_ref, p_ref.shape)
    if not last:
        add_rims((near, far, side), p_in, q_in, a_ref, b_ref, p_ref, q_ref)
        put_rims_of(facts_ref, p_ref, *out_refs)
        return
    p_out, q_out, sem = out_refs
    nx, ny, _ = p_ref.shape
    for rows, term in ((slice(0, REACH), near), (slice(nx - REACH, nx), far)):
        p_ref[rows] = p_in[rows] + a_ref[rows] * term
        q_ref[rows] = q_in[rows] + b_ref[rows] * term
    copies = []
    for i in range(nx // XT):
        rows = slice(i * XT, (i + 1) * XT)
        for cells, term in ((slice(0, 8), side[rows, 0:8]), (slice(ny - 8, ny), side[rows, 8:16])):
            p_ref[rows, cells] += a_ref[rows, cells] * term
            q_ref[rows, cells] += b_ref[rows, cells] * term
        for k, (ref, out) in enumerate(((p_ref, p_out), (q_ref, q_out))):
            copies.append(pltpu.make_async_copy(ref.at[rows], out.at[rows], sem.at[k, i]))
            copies[-1].start()
    for copy in copies:
        copy.wait()


def call(kernel, name, scalars, arrays, out, scratch=(), aliases=None, hbm=(), hbm_out=0, smem_out=0):
    vmem = pl.BlockSpec(memory_space=pltpu.VMEM)
    smem = pl.BlockSpec(memory_space=pltpu.SMEM)
    anywhere = pl.BlockSpec(memory_space=pl.ANY)
    return pl.pallas_call(
        kernel,
        out_shape=out,
        in_specs=[smem] * len(scalars) + [vmem] * len(arrays) + [anywhere] * len(hbm),
        out_specs=[vmem] * (len(out) - hbm_out - smem_out) + [anywhere] * hbm_out + [smem] * smem_out,
        scratch_shapes=scratch,
        input_output_aliases=aliases or {},
        compiler_params=pltpu.CompilerParams(vmem_limit_bytes=VMEM_LIMIT),
        name=name,
    )(*in_hbm(*scalars), *arrays, *hbm)


def in_vmem(*arrays):
    return [pltpu.with_memory_space_constraint(a, pltpu.VMEM) for a in arrays]


def in_hbm(*arrays):
    return [pltpu.with_memory_space_constraint(a, pltpu.HBM) for a in arrays]


def on_device(velocity, epsilon, delta, anchors, sources, wavelet, p_now, p_prev, q_now, q_prev):
    p, pb, q, qb = p_now[0], p_prev[0], q_now[0], q_prev[0]
    nx, ny, nz = p.shape
    f32, bf16 = jnp.float32, jnp.bfloat16
    ids = jnp.stack([lax.axis_index(name) for name in ("shot", "gx", "gy")])
    block = pltpu.VMEM((nx, ny, nz), f32)
    x_rim, y_rim = (pltpu.VMEM(((REACH + 1) * n, nz), bf16) for n in (ny, nx))
    rim_shapes = [x_rim] * len(swaps(lax.axis_size("gx"))) + [y_rim] * len(swaps(lax.axis_size("gy")))
    padded = [pltpu.VMEM((nx + 2 * REACH, ny, nz), bf16)] * 2
    dz = jnp.asarray(depth_matrix(nz), bf16)
    dh = jnp.asarray(plane_matrix(ny), bf16)
    ds = jnp.asarray(side_matrix(nx), bf16)
    facts, waves, *index = call(
        functools.partial(facts_kernel, lax.axis_size("gx"), p.shape), "facts", [ids, anchors, sources, wavelet], [],
        [pltpu.VMEM((8, nz), jnp.int32), pltpu.VMEM((STEPS, nz), f32), *[jax.ShapeDtypeStruct((1,), jnp.int32)] * 2],
        smem_out=2,
    )
    edges = call(
        edge_kernel, "edges", [], in_vmem(facts), rim_shapes,
        [pltpu.VMEM((REACH, ny, nz), f32)] * 2 + [pltpu.VMEM((nx, 8, nz), f32)] * 2 + [pltpu.SemaphoreType.DMA((4,))],
        hbm=in_hbm(p),
    )
    rims = exchange(edges)
    windows, rims = model_windows(ids, anchors, (velocity, epsilon, delta), index, rims)
    p0, q0 = p, q
    p, q, a, b, c, *rims = call(
        functools.partial(first_kernel, len(rims)), "first", [ids, anchors], in_vmem(facts, waves, p0, q0, dh, dz, ds),
        [block] * 5 + rim_shapes, padded + [block] * 2 + [pltpu.VMEM((nx, ny, nz), bf16)] * 3 + rim_shapes
        + [pltpu.SemaphoreType.DMA((5, nx // XT)), pltpu.SemaphoreType.DMA((len(rims),))],
        hbm=in_hbm(pb, qb) + windows + in_hbm(*rims),
    )
    pb, qb = p0, q0
    for step in range(1, STEPS):
        rims = exchange(rims)
        p_new, q_new = call(
            functools.partial(inner_kernel, step), f"inner_{step}", [],
            in_vmem(facts, waves, p, pb, q, qb, a, b, c, dh, dz), [block] * 2, padded,
        )
        last = step == STEPS - 1
        whole = jax.ShapeDtypeStruct((nx, ny, nz), f32)
        out = call(
            functools.partial(rim_kernel, len(rims), last), f"rims_{step}", [], in_vmem(facts, p_new, q_new, a, b, *rims, ds),
            [block] * 2 + ([whole] * 2 if last else rim_shapes),
            [pltpu.SemaphoreType.DMA((2, nx // XT))] if last else [],
            {1: 0, 2: 1},
            hbm_out=2 if last else 0,
        )
        pb, qb = p, q
        p, q, *rims = out
    return rims[0][None], rims[1][None]


def solution(mesh):
    model = P(("shot", "gx"), "gy", None)
    field = P("shot", "gx", "gy", None)
    return jax.shard_map(
        on_device,
        mesh=mesh,
        in_specs=(model, model, model, P(), P("shot", None), P("shot", None)) + (field,) * 4,
        out_specs=(field, field),
        check_vma=False,
    )
```

profile of v0, /device:TPU:0, one launch (start us, length us, event | category | flops | bytes accessed | tf_op | source)
XLA Modules:
  0.0 90.4 jit_solution(12817958598181498841)
XLA Ops:
  0.6 0.5 collective-permute-start.153
  1.1 0.1 collective-permute-start.154
  1.2 2.9 %collective-permute-start.155 = (bf16[32,32,256]{2,1,0:T(8,128)(2,1)}, bf16[32,32,256]{2,1,0:T(8,128)(2,1)S(1)}, u32[]{:S(2)}, u32[]{:S(2)}) collective-permute-start(bf16[32,32,256]{2,1,0:T(8,128)(2,1)} %refs_0_.1), channel_id=1, source_target_pairs={{0,16},{8,24},{16,0},{24,8},{1,17},{9,25},{17,1},{25,9},{2,18},{10... | collective-permute-start | bytes 1572872 | tf_op jit(solution)/shard_map/ppermute | solution.py:108
  4.1 0.7 pad_add_fusion.ids_ref
  4.8 1.2 %facts.1 = (s32[8,256]{1,0:T(8,128)S(1)}, f32[4,256]{1,0:T(4,128)S(1)}, s32[1]{0:T(128)}, s32[1]{0:T(128)}) custom-call(s32[3]{0:T(128)} %pad_add_fusion.ids_ref, s32[4]{0:T(128)} %anchors_ref.13, s32[1,3]{1,0:T(1,128)} %sources_ref.1, f32[1,4]{1,0:T(1,128)} %wavelet_ref.1), custom_call_target="tpu_custom_call" | custom-call | tf_op jit(solution)/shard_map/facts/pallas_call | solution.py:386
  6.0 0.0 copy-start.6
  6.0 1.4 %edges.1 = (bf16[160,256]{1,0:T(8,128)(2,1)S(1)}, bf16[160,256]{1,0:T(8,128)(2,1)S(1)}, bf16[160,256]{1,0:T(8,128)(2,1)S(1)}) custom-call(s32[8,256]{1,0:T(8,128)S(1)} %get-tuple-element.271.facts_ref, f32[32,32,256]{2,1,0:T(8,128)} %bitcast.11), custom_call_target="tpu_custom_call" | custom-call | tf_op jit(solution)/shard_map/edges/pallas_call | solution.py:386
  7.4 1.6 %collective-permute-start.156 = (bf16[160,256]{1,0:T(8,128)(2,1)S(1)}, bf16[160,256]{1,0:T(8,128)(2,1)S(1)}, u32[]{:S(2)}, u32[]{:S(2)}) collective-permute-start(bf16[160,256]{1,0:T(8,128)(2,1)S(1)} %get-tuple-element.275), channel_id=1, source_target_pairs={{0,2},{2,0},{4,6},{6,4},{1,3},{3,1},{5,7},{7,5},{8,10},{10,8},{12,... | collective-permute-start | bytes 245768 | tf_op jit(solution)/shard_map/ppermute | solution.py:137
  9.1 0.7 collective-permute-start.157
  9.7 0.0 collective-permute-done.153.other_ref
  9.7 0.0 copy-start.5
  9.7 0.0 copy-start.7
  9.8 1.6 %collective-permute-start.158 = (bf16[160,256]{1,0:T(8,128)(2,1)S(1)}, bf16[160,256]{1,0:T(8,128)(2,1)S(1)}, u32[]{:S(2)}, u32[]{:S(2)}) collective-permute-start(bf16[160,256]{1,0:T(8,128)(2,1)S(1)} %get-tuple-element.277), channel_id=1, source_target_pairs={{0,1},{1,0},{2,3},{3,2},{4,5},{5,4},{6,7},{7,6},{8,9},{9,8},{10,11... | collective-permute-start | bytes 245768 | tf_op jit(solution)/shard_map/ppermute | solution.py:137
  11.3 1.6 %pick_1.1 = (bf16[32,32,256]{2,1,0:T(8,128)(2,1)}, bf16[32,32,256]{2,1,0:T(8,128)(2,1)S(1)}) custom-call(s32[3]{0:T(128)} %pad_add_fusion.ids_ref, s32[4]{0:T(128)} %anchors_ref.13, bf16[32,32,256]{2,1,0:T(8,128)(2,1)S(1)} %copy-done.6, bf16[32,32,256]{2,1,0:T(8,128)(2,1)S(1)} %collective-permute-done.153.other_ref), custom_call_target="tpu_custom_call" | custom-call | tf_op jit(solution)/shard_map/pick_1/pallas_call | solution.py:386
  12.9 0.0 collective-permute-start.161
  13.0 0.8 pick_2.1
  13.8 0.4 collective-permute-done.158.refs_7_
  14.3 2.3 %collective-permute-done.155.refs_1_ = bf16[32,32,256]{2,1,0:T(8,128)(2,1)S(1)} collective-permute-done((bf16[32,32,256]{2,1,0:T(8,128)(2,1)}, bf16[32,32,256]{2,1,0:T(8,128)(2,1)S(1)}, u32[]{:S(2)}, u32[]{:S(2)}) %collective-permute-start.155) | collective-permute-done | bytes 524320 | tf_op jit(solution)/shard_map/ppermute | solution.py:108
  16.5 1.7 %collective-permute-start.160 = (bf16[32,32,256]{2,1,0:T(8,128)(2,1)}, bf16[32,32,256]{2,1,0:T(8,128)(2,1)S(1)}, u32[]{:S(2)}, u32[]{:S(2)}) collective-permute-start(bf16[32,32,256]{2,1,0:T(8,128)(2,1)} %get-tuple-element.281), channel_id=1, source_target_pairs={{0,16},{8,24},{16,0},{24,8},{1,17},{9,25},{17,1},{25,9},{2,18},{10... | collective-permute-start | bytes 1572872 | tf_op jit(solution)/shard_map/ppermute | solution.py:118
  18.3 0.3 collective-permute-start.159
  19.9 0.0 collective-permute-done.162.refs_3_
  19.9 0.8 join_0.1
  20.7 11.9 %conditional.3 = (bf16[35,32,256]{2,1,0:T(8,128)(2,1)}) conditional(s32[]{:T(128)} %bitcast.7, bf16[32,32,256]{2,1,0:T(8,128)(2,1)S(1)} %join_0.1, bf16[32,32,256]{2,1,0:T(8,128)(2,1)S(1)} %join_0.1, bf16[32,32,256]{2,1,0:T(8,128)(2,1)S(1)} %join_0.1, bf16[32,32,256]{2,1,0:T(8,128)(2,1)S(1)} %join_0.1, ...), branch_computations={%region_0.0_spmd, %region_1.0_spmd, %region_2.0_spmd, %region_3.0_... | conditional | flops 286720 | bytes 4587608 | solution.py:106
  20.8 2.4 %collective-permute-start.49 = (bf16[31,32,256]{2,1,0:T(8,128)(2,1)S(1)}, bf16[31,32,256]{2,1,0:T(8,128)(2,1)S(1)}, u32[]{:S(2)}, u32[]{:S(2)}) collective-permute-start(bf16[31,32,256]{2,1,0:T(8,128)(2,1)S(1)} %slice.405), channel_id=1, source_target_pairs={{0,2},{2,4},{4,6},{6,0},{1,3},{3,5},{5,7},{7,1},{8,10},{10,12},{12... | collective-permute-start | bytes 1523720 | tf_op jit(solution)/shard_map/cond/branch_28_fun/ppermute | solution.py:76
  23.2 8.5 %collective-permute-done.49 = bf16[31,32,256]{2,1,0:T(8,128)(2,1)S(1)} collective-permute-done((bf16[31,32,256]{2,1,0:T(8,128)(2,1)S(1)}, bf16[31,32,256]{2,1,0:T(8,128)(2,1)S(1)}, u32[]{:S(2)}, u32[]{:S(2)}) %collective-permute-start.49) | collective-permute-done | bytes 507936 | tf_op jit(solution)/shard_map/cond/branch_28_fun/ppermute | solution.py:76
  31.7 0.9 pad_maximum_fusion.24
  32.6 0.7 join_1.1
  33.3 0.9 conditional.4
  33.4 0.9 concatenate.252
  34.2 8.1 %collective-permute-done.159.refs_1_ = bf16[32,32,256]{2,1,0:T(8,128)(2,1)S(1)} collective-permute-done((bf16[32,32,256]{2,1,0:T(8,128)(2,1)S(1)}, bf16[32,32,256]{2,1,0:T(8,128)(2,1)S(1)}, u32[]{:S(2)}, u32[]{:S(2)}) %collective-permute-start.159) | collective-permute-done | bytes 524320 | tf_op jit(solution)/shard_map/ppermute | solution.py:118
  42.3 3.7 %collective-permute-start.163 = (bf16[35,32,256]{2,1,0:T(8,128)(2,1)}, bf16[35,32,256]{2,1,0:T(8,128)(2,1)S(1)}, u32[]{:S(2)}, u32[]{:S(2)}) collective-permute-start(bf16[35,32,256]{2,1,0:T(8,128)(2,1)} %get-tuple-element.321), channel_id=1, source_target_pairs={{0,16},{8,24},{16,0},{24,8},{1,17},{9,25},{17,1},{25,9},{2,18},{10... | collective-permute-start | bytes 1720328 | tf_op jit(solution)/shard_map/ppermute | solution.py:124
  46.0 0.7 join_2.1
  46.7 0.0 copy-start
  46.8 0.0 copy-start.1
  46.8 0.0 copy-start.2
  46.8 0.0 copy-start.3
  46.8 0.0 copy-start.4
  46.8 0.9 conditional.5
  46.8 0.9 concatenate.288
  47.7 11.8 %collective-permute-done.163.refs_2_ = bf16[35,32,256]{2,1,0:T(8,128)(2,1)S(1)} collective-permute-done((bf16[35,32,256]{2,1,0:T(8,128)(2,1)}, bf16[35,32,256]{2,1,0:T(8,128)(2,1)S(1)}, u32[]{:S(2)}, u32[]{:S(2)}) %collective-permute-start.163) | collective-permute-done | bytes 573472 | tf_op jit(solution)/shard_map/ppermute | solution.py:124
  59.6 5.0 %first.1 = (f32[32,32,256]{2,1,0:T(8,128)S(1)}, f32[32,32,256]{2,1,0:T(8,128)S(1)}, f32[32,32,256]{2,1,0:T(8,128)S(1)}, f32[32,32,256]{2,1,0:T(8,128)S(1)}, f32[...) custom-call(s32[3]{0:T(128)} %pad_add_fusion.ids_ref, ...), custom_call_target="tpu_custom_call" | custom-call | tf_op jit(solution)/shard_map/first/pallas_call | solution.py:386
  64.6 0.1 collective-permute-start.164
  64.7 0.7 collective-permute-start.165
  65.4 1.5 %collective-permute-start.166 = (bf16[160,256]{1,0:T(8,128)(2,1)S(1)}, bf16[160,256]{1,0:T(8,128)(2,1)S(1)}, u32[]{:S(2)}, u32[]{:S(2)}) collective-permute-start(bf16[160,256]{1,0:T(8,128)(2,1)S(1)} %get-tuple-element.304), channel_id=1, source_target_pairs={{0,1},{1,0},{2,3},{3,2},{4,5},{5,4},{6,7},{7,6},{8,9},{9,8},{10,11... | collective-permute-start | bytes 245768 | tf_op jit(solution)/shard_map/ppermute | solution.py:137
  66.8 2.1 %inner_1.1 = (f32[32,32,256]{2,1,0:T(8,128)S(1)}, f32[32,32,256]{2,1,0:T(8,128)S(1)}) custom-call(s32[8,256]{1,0:T(8,128)S(1)} %get-tuple-element.271.facts_ref, f32[4,256]{1,0:T(4,128)S(1)} %get-tuple-element.272.wave_ref, f32[32,32,256]{2,1,0:T(8,128)S(1)} %get-tuple-element.295.p_ref.pb_ref, f32[32,32,256]{2,1,0:T(8,128)S(1)} %bitcast.13, ...), custom_call_target="tpu_custom_call" | custom-call | tf_op jit(solution)/shard_map/inner_1/pallas_call | solution.py:386
  69.0 0.4 collective-permute-done.164.refs_0_
  69.3 0.0 collective-permute-done.165.refs_1_
  69.3 1.4 %collective-permute-done.166.refs_2_ = bf16[160,256]{1,0:T(8,128)(2,1)S(1)} collective-permute-done((bf16[160,256]{1,0:T(8,128)(2,1)S(1)}, bf16[160,256]{1,0:T(8,128)(2,1)S(1)}, u32[]{:S(2)}, u32[]{:S(2)}) %collective-permute-start.166) | collective-permute-done | bytes 81952 | tf_op jit(solution)/shard_map/ppermute | solution.py:137
  70.7 0.6 rims_1.1
  71.3 3.1 %collective-permute-start.167 = (bf16[160,256]{1,0:T(8,128)(2,1)S(1)}, bf16[160,256]{1,0:T(8,128)(2,1)S(1)}, u32[]{:S(2)}, u32[]{:S(2)}) collective-permute-start(bf16[160,256]{1,0:T(8,128)(2,1)S(1)} %get-tuple-element.309), channel_id=1, source_target_pairs={{0,2},{2,0},{4,6},{6,4},{1,3},{3,1},{5,7},{7,5},{8,10},{10,8},{12,... | collective-permute-start | bytes 245768 | tf_op jit(solution)/shard_map/ppermute | solution.py:137
  74.4 0.7 collective-permute-start.168
  75.1 1.6 %collective-permute-start.169 = (bf16[160,256]{1,0:T(8,128)(2,1)S(1)}, bf16[160,256]{1,0:T(8,128)(2,1)S(1)}, u32[]{:S(2)}, u32[]{:S(2)}) collective-permute-start(bf16[160,256]{1,0:T(8,128)(2,1)S(1)} %get-tuple-element.311), channel_id=1, source_target_pairs={{0,1},{1,0},{2,3},{3,2},{4,5},{5,4},{6,7},{7,6},{8,9},{9,8},{10,11... | collective-permute-start | bytes 245768 | tf_op jit(solution)/shard_map/ppermute | solution.py:137
  76.7 2.1 %inner_2.1 = (f32[32,32,256]{2,1,0:T(8,128)S(1)}, f32[32,32,256]{2,1,0:T(8,128)S(1)}) custom-call(s32[8,256]{1,0:T(8,128)S(1)} %get-tuple-element.271.facts_ref, f32[4,256]{1,0:T(4,128)S(1)} %get-tuple-element.272.wave_ref, f32[32,32,256]{2,1,0:T(8,128)S(1)} %get-tuple-element.305.p_ref.pb_ref, f32[32,32,256]{2,1,0:T(8,128)S(1)} %get-tuple-element.295.p_ref.pb_ref, ...), custom_call_target="tpu_custom_call" | custom-call | tf_op jit(solution)/shard_map/inner_2/pallas_call | solution.py:386
  78.8 0.0 collective-permute-done.167.refs_0_
  78.8 0.0 collective-permute-done.168.refs_1_
  78.8 1.0 %collective-permute-done.169.refs_2_ = bf16[160,256]{1,0:T(8,128)(2,1)S(1)} collective-permute-done((bf16[160,256]{1,0:T(8,128)(2,1)S(1)}, bf16[160,256]{1,0:T(8,128)(2,1)S(1)}, u32[]{:S(2)}, u32[]{:S(2)}) %collective-permute-start.169) | collective-permute-done | bytes 81952 | tf_op jit(solution)/shard_map/ppermute | solution.py:137
  79.9 0.6 rims_2.1
  80.4 2.9 %collective-permute-start.170 = (bf16[160,256]{1,0:T(8,128)(2,1)S(1)}, bf16[160,256]{1,0:T(8,128)(2,1)S(1)}, u32[]{:S(2)}, u32[]{:S(2)}) collective-permute-start(bf16[160,256]{1,0:T(8,128)(2,1)S(1)} %get-tuple-element.316), channel_id=1, source_target_pairs={{0,2},{2,0},{4,6},{6,4},{1,3},{3,1},{5,7},{7,5},{8,10},{10,8},{12,... | collective-permute-start | bytes 245768 | tf_op jit(solution)/shard_map/ppermute | solution.py:137
  83.4 0.7 collective-permute-start.171
  84.0 1.6 %collective-permute-start.172 = (bf16[160,256]{1,0:T(8,128)(2,1)S(1)}, bf16[160,256]{1,0:T(8,128)(2,1)S(1)}, u32[]{:S(2)}, u32[]{:S(2)}) collective-permute-start(bf16[160,256]{1,0:T(8,128)(2,1)S(1)} %get-tuple-element.318), channel_id=1, source_target_pairs={{0,1},{1,0},{2,3},{3,2},{4,5},{5,4},{6,7},{7,6},{8,9},{9,8},{10,11... | collective-permute-start | bytes 245768 | tf_op jit(solution)/shard_map/ppermute | solution.py:137
  85.6 2.1 %inner_3.1 = (f32[32,32,256]{2,1,0:T(8,128)S(1)}, f32[32,32,256]{2,1,0:T(8,128)S(1)}) custom-call(s32[8,256]{1,0:T(8,128)S(1)} %get-tuple-element.271.facts_ref, f32[4,256]{1,0:T(4,128)S(1)} %get-tuple-element.272.wave_ref, f32[32,32,256]{2,1,0:T(8,128)S(1)} %get-tuple-element.312.p_ref, f32[32,32,256]{2,1,0:T(8,128)S(1)} %get-tuple-element.305.p_ref.pb_ref, ...), custom_call_target="tpu_custom_call" | custom-call | tf_op jit(solution)/shard_map/inner_3/pallas_call | solution.py:386
  87.7 0.0 collective-permute-done.170.refs_0_
  87.8 0.8 collective-permute-done.172.refs_2_
  88.5 1.7 %rims_3.1 = (f32[32,32,256]{2,1,0:T(8,128)S(1)}, f32[32,32,256]{2,1,0:T(8,128)S(1)}, f32[32,32,256]{2,1,0:T(8,128)}, f32[32,32,256]{2,1,0:T(8,128)}) custom-call(s32[8,256]{1,0:T(8,128)S(1)} %get-tuple-element.271.facts_ref, f32[32,32,256]{2,1,0:T(8,128)S(1)} %get-tuple-element.314.p_in, ...), custom_call_target="tpu_custom_call", output_to_operand_aliasing={{0}: (1, {}), {1}: (2, {})} | custom-call | tf_op jit(solution)/shard_map/rims_3/pallas_call | solution.py:386
  (23 shorter events, 0.1 us)
Async XLA Ops:
  0.6 9.1 %collective-permute-start.153 = (bf16[32,32,256]{2,1,0:T(8,128)(2,1)}, bf16[32,32,256]{2,1,0:T(8,128)(2,1)S(1)}, u32[]{:S(2)}, u32[]{:S(2)}) collective-permute-start(bf16[32,32,256]{2,1,0:T(8,128)(2,1)} %field_ref.2), channel_id=1, source_target_pairs={{0,8},{8,0},{16,24},{24,16},{1,9},{9,1},{17,25},{25,17},{2,10},{10... | collective-permute-start | bytes 1572872 | tf_op jit(solution)/shard_map/ppermute | solution.py:109
  1.1 11.8 %collective-permute-start.154 = (bf16[32,32,256]{2,1,0:T(8,128)(2,1)}, bf16[32,32,256]{2,1,0:T(8,128)(2,1)S(1)}, u32[]{:S(2)}, u32[]{:S(2)}) collective-permute-start(bf16[32,32,256]{2,1,0:T(8,128)(2,1)} %field_ref.3), channel_id=1, source_target_pairs={{0,8},{8,0},{16,24},{24,16},{1,9},{9,1},{17,25},{25,17},{2,10},{10... | collective-permute-start | bytes 1572872 | tf_op jit(solution)/shard_map/ppermute | solution.py:109
  1.2 15.3 %collective-permute-start.155 = (bf16[32,32,256]{2,1,0:T(8,128)(2,1)}, bf16[32,32,256]{2,1,0:T(8,128)(2,1)S(1)}, u32[]{:S(2)}, u32[]{:S(2)}) collective-permute-start(bf16[32,32,256]{2,1,0:T(8,128)(2,1)} %refs_0_.1), channel_id=1, source_target_pairs={{0,16},{8,24},{16,0},{24,8},{1,17},{9,25},{17,1},{25,9},{2,18},{10... | collective-permute-start | bytes 1572872 | tf_op jit(solution)/shard_map/ppermute | solution.py:108
  6.0 5.3 %copy-start.6 = (bf16[32,32,256]{2,1,0:T(8,128)(2,1)S(1)}, bf16[32,32,256]{2,1,0:T(8,128)(2,1)}, u32[]{:S(2)}) copy-start(bf16[32,32,256]{2,1,0:T(8,128)(2,1)} %field_ref.2) | copy-start | bytes 1572868
  7.4 6.4 %collective-permute-start.156 = (bf16[160,256]{1,0:T(8,128)(2,1)S(1)}, bf16[160,256]{1,0:T(8,128)(2,1)S(1)}, u32[]{:S(2)}, u32[]{:S(2)}) collective-permute-start(bf16[160,256]{1,0:T(8,128)(2,1)S(1)} %get-tuple-element.275), channel_id=1, source_target_pairs={{0,2},{2,0},{4,6},{6,4},{1,3},{3,1},{5,7},{7,5},{8,10},{10,8},{12,... | collective-permute-start | bytes 245768 | tf_op jit(solution)/shard_map/ppermute | solution.py:137
  9.1 4.7 %collective-permute-start.157 = (bf16[160,256]{1,0:T(8,128)(2,1)S(1)}, bf16[160,256]{1,0:T(8,128)(2,1)S(1)}, u32[]{:S(2)}, u32[]{:S(2)}) collective-permute-start(bf16[160,256]{1,0:T(8,128)(2,1)S(1)} %get-tuple-element.276), channel_id=1, source_target_pairs={{2,4},{4,2},{3,5},{5,3},{10,12},{12,10},{11,13},{13,11},{18,20},{2... | collective-permute-start | bytes 245768 | tf_op jit(solution)/shard_map/ppermute | solution.py:137
  9.7 3.2 %copy-start.5 = (bf16[32,32,256]{2,1,0:T(8,128)(2,1)S(1)}, bf16[32,32,256]{2,1,0:T(8,128)(2,1)}, u32[]{:S(2)}) copy-start(bf16[32,32,256]{2,1,0:T(8,128)(2,1)} %refs_0_.1) | copy-start | bytes 1572868
  9.7 3.2 %copy-start.7 = (bf16[32,32,256]{2,1,0:T(8,128)(2,1)S(1)}, bf16[32,32,256]{2,1,0:T(8,128)(2,1)}, u32[]{:S(2)}) copy-start(bf16[32,32,256]{2,1,0:T(8,128)(2,1)} %field_ref.3) | copy-start | bytes 1572868
  9.8 4.5 %collective-permute-start.158 = (bf16[160,256]{1,0:T(8,128)(2,1)S(1)}, bf16[160,256]{1,0:T(8,128)(2,1)S(1)}, u32[]{:S(2)}, u32[]{:S(2)}) collective-permute-start(bf16[160,256]{1,0:T(8,128)(2,1)S(1)} %get-tuple-element.277), channel_id=1, source_target_pairs={{0,1},{1,0},{2,3},{3,2},{4,5},{5,4},{6,7},{7,6},{8,9},{9,8},{10,11... | collective-permute-start | bytes 245768 | tf_op jit(solution)/shard_map/ppermute | solution.py:137
  12.9 6.9 %collective-permute-start.161 = (bf16[32,32,256]{2,1,0:T(8,128)(2,1)S(1)}, bf16[32,32,256]{2,1,0:T(8,128)(2,1)S(1)}, u32[]{:S(2)}, u32[]{:S(2)}) collective-permute-start(bf16[32,32,256]{2,1,0:T(8,128)(2,1)S(1)} %copy-done.5), channel_id=1, source_target_pairs={{0,8},{8,0},{16,24},{24,16},{1,9},{9,1},{17,25},{25,17},{2,10},{10... | collective-permute-start | bytes 1572872 | tf_op jit(solution)/shard_map/ppermute | solution.py:109
  13.8 6.9 %copy-start.8 = (bf16[160,256]{1,0:T(8,128)(2,1)}, bf16[160,256]{1,0:T(8,128)(2,1)S(1)}, u32[]{:S(2)}) copy-start(bf16[160,256]{1,0:T(8,128)(2,1)S(1)} %collective-permute-done.156.refs_5_) | copy-start | bytes 245764
  13.8 6.1 %copy-start.9 = (bf16[160,256]{1,0:T(8,128)(2,1)}, bf16[160,256]{1,0:T(8,128)(2,1)S(1)}, u32[]{:S(2)}) copy-start(bf16[160,256]{1,0:T(8,128)(2,1)S(1)} %collective-permute-done.157.refs_6_) | copy-start | bytes 245764
  14.3 5.6 %copy-start.10 = (bf16[160,256]{1,0:T(8,128)(2,1)}, bf16[160,256]{1,0:T(8,128)(2,1)S(1)}, u32[]{:S(2)}) copy-start(bf16[160,256]{1,0:T(8,128)(2,1)S(1)} %collective-permute-done.158.refs_7_) | copy-start | bytes 245764
  16.5 3.4 %collective-permute-start.162 = (bf16[32,32,256]{2,1,0:T(8,128)(2,1)S(1)}, bf16[32,32,256]{2,1,0:T(8,128)(2,1)S(1)}, u32[]{:S(2)}, u32[]{:S(2)}) collective-permute-start(bf16[32,32,256]{2,1,0:T(8,128)(2,1)S(1)} %collective-permute-done.155.refs_1_), channel_id=1, source_target_pairs={{0,8},{8,0},{16,24},{24,16},{1,9},{9,1},{17,25},{25,17},{2,10},{10... | collective-permute-start | bytes 1572872 | tf_op jit(solution)/shard_map/ppermute | solution.py:119
  16.5 16.1 %collective-permute-start.160 = (bf16[32,32,256]{2,1,0:T(8,128)(2,1)}, bf16[32,32,256]{2,1,0:T(8,128)(2,1)S(1)}, u32[]{:S(2)}, u32[]{:S(2)}) collective-permute-start(bf16[32,32,256]{2,1,0:T(8,128)(2,1)} %get-tuple-element.281), channel_id=1, source_target_pairs={{0,16},{8,24},{16,0},{24,8},{1,17},{9,25},{17,1},{25,9},{2,18},{10... | collective-permute-start | bytes 1572872 | tf_op jit(solution)/shard_map/ppermute | solution.py:118
  18.3 24.0 %collective-permute-start.159 = (bf16[32,32,256]{2,1,0:T(8,128)(2,1)S(1)}, bf16[32,32,256]{2,1,0:T(8,128)(2,1)S(1)}, u32[]{:S(2)}, u32[]{:S(2)}) collective-permute-start(bf16[32,32,256]{2,1,0:T(8,128)(2,1)S(1)} %get-tuple-element.280), channel_id=1, source_target_pairs={{0,16},{8,24},{16,0},{24,8},{1,17},{9,25},{17,1},{25,9},{2,18},{10... | collective-permute-start | bytes 1572872 | tf_op jit(solution)/shard_map/ppermute | solution.py:118
  20.8 10.9 %collective-permute-start.49 = (bf16[31,32,256]{2,1,0:T(8,128)(2,1)S(1)}, bf16[31,32,256]{2,1,0:T(8,128)(2,1)S(1)}, u32[]{:S(2)}, u32[]{:S(2)}) collective-permute-start(bf16[31,32,256]{2,1,0:T(8,128)(2,1)S(1)} %slice.405), channel_id=1, source_target_pairs={{0,2},{2,4},{4,6},{6,0},{1,3},{3,5},{5,7},{7,1},{8,10},{10,12},{12... | collective-permute-start | bytes 1523720 | tf_op jit(solution)/shard_map/cond/branch_28_fun/ppermute | solution.py:76
  42.3 17.2 %collective-permute-start.163 = (bf16[35,32,256]{2,1,0:T(8,128)(2,1)}, bf16[35,32,256]{2,1,0:T(8,128)(2,1)S(1)}, u32[]{:S(2)}, u32[]{:S(2)}) collective-permute-start(bf16[35,32,256]{2,1,0:T(8,128)(2,1)} %get-tuple-element.321), channel_id=1, source_target_pairs={{0,16},{8,24},{16,0},{24,8},{1,17},{9,25},{17,1},{25,9},{2,18},{10... | collective-permute-start | bytes 1720328 | tf_op jit(solution)/shard_map/ppermute | solution.py:124
  46.7 12.8 %copy-start = (f32[1,32,32,256]{3,2,1,0:T(8,128)S(1)}, f32[1,32,32,256]{3,2,1,0:T(8,128)}, u32[]{:S(2)}) copy-start(f32[1,32,32,256]{3,2,1,0:T(8,128)} %param.127) | copy-start | bytes 3145732
  46.8 12.8 %copy-start.1 = (bf16[512,320]{1,0:T(8,128)(2,1)S(1)}, bf16[512,320]{1,0:T(8,128)(2,1)}, u32[]{:S(2)}) copy-start(bf16[512,320]{1,0:T(8,128)(2,1)} %constant.51.clone.ds_ref.refs_3_) | copy-start | bytes 983044
  46.8 12.8 %copy-start.2 = (bf16[256,512]{1,0:T(8,128)(2,1)S(1)}, bf16[256,512]{1,0:T(8,128)(2,1)}, u32[]{:S(2)}) copy-start(bf16[256,512]{1,0:T(8,128)(2,1)} %constant.50.clone.dh_ref) | copy-start | bytes 786436
  46.8 12.8 %copy-start.3 = (f32[1,32,32,256]{3,2,1,0:T(8,128)S(1)}, f32[1,32,32,256]{3,2,1,0:T(8,128)}, u32[]{:S(2)}) copy-start(f32[1,32,32,256]{3,2,1,0:T(8,128)} %param.129) | copy-start | bytes 3145732
  46.8 12.8 %copy-start.4 = (bf16[256,256]{1,0:T(8,128)(2,1)S(1)}, bf16[256,256]{1,0:T(8,128)(2,1)}, u32[]{:S(2)}) copy-start(bf16[256,256]{1,0:T(8,128)(2,1)} %constant.49.clone.dz_ref) | copy-start | bytes 393220
  64.6 4.7 %collective-permute-start.164 = (bf16[160,256]{1,0:T(8,128)(2,1)S(1)}, bf16[160,256]{1,0:T(8,128)(2,1)S(1)}, u32[]{:S(2)}, u32[]{:S(2)}) collective-permute-start(bf16[160,256]{1,0:T(8,128)(2,1)S(1)} %get-tuple-element.302), channel_id=1, source_target_pairs={{0,2},{2,0},{4,6},{6,4},{1,3},{3,1},{5,7},{7,5},{8,10},{10,8},{12,... | collective-permute-start | bytes 245768 | tf_op jit(solution)/shard_map/ppermute | solution.py:137
  64.7 4.7 %collective-permute-start.165 = (bf16[160,256]{1,0:T(8,128)(2,1)S(1)}, bf16[160,256]{1,0:T(8,128)(2,1)S(1)}, u32[]{:S(2)}, u32[]{:S(2)}) collective-permute-start(bf16[160,256]{1,0:T(8,128)(2,1)S(1)} %get-tuple-element.303), channel_id=1, source_target_pairs={{2,4},{4,2},{3,5},{5,3},{10,12},{12,10},{11,13},{13,11},{18,20},{2... | collective-permute-start | bytes 245768 | tf_op jit(solution)/shard_map/ppermute | solution.py:137
  65.4 5.4 %collective-permute-start.166 = (bf16[160,256]{1,0:T(8,128)(2,1)S(1)}, bf16[160,256]{1,0:T(8,128)(2,1)S(1)}, u32[]{:S(2)}, u32[]{:S(2)}) collective-permute-start(bf16[160,256]{1,0:T(8,128)(2,1)S(1)} %get-tuple-element.304), channel_id=1, source_target_pairs={{0,1},{1,0},{2,3},{3,2},{4,5},{5,4},{6,7},{7,6},{8,9},{9,8},{10,11... | collective-permute-start | bytes 245768 | tf_op jit(solution)/shard_map/ppermute | solution.py:137
  71.3 7.5 %collective-permute-start.167 = (bf16[160,256]{1,0:T(8,128)(2,1)S(1)}, bf16[160,256]{1,0:T(8,128)(2,1)S(1)}, u32[]{:S(2)}, u32[]{:S(2)}) collective-permute-start(bf16[160,256]{1,0:T(8,128)(2,1)S(1)} %get-tuple-element.309), channel_id=1, source_target_pairs={{0,2},{2,0},{4,6},{6,4},{1,3},{3,1},{5,7},{7,5},{8,10},{10,8},{12,... | collective-permute-start | bytes 245768 | tf_op jit(solution)/shard_map/ppermute | solution.py:137
  74.4 4.4 %collective-permute-start.168 = (bf16[160,256]{1,0:T(8,128)(2,1)S(1)}, bf16[160,256]{1,0:T(8,128)(2,1)S(1)}, u32[]{:S(2)}, u32[]{:S(2)}) collective-permute-start(bf16[160,256]{1,0:T(8,128)(2,1)S(1)} %get-tuple-element.310), channel_id=1, source_target_pairs={{2,4},{4,2},{3,5},{5,3},{10,12},{12,10},{11,13},{13,11},{18,20},{2... | collective-permute-start | bytes 245768 | tf_op jit(solution)/shard_map/ppermute | solution.py:137
  75.1 4.8 %collective-permute-start.169 = (bf16[160,256]{1,0:T(8,128)(2,1)S(1)}, bf16[160,256]{1,0:T(8,128)(2,1)S(1)}, u32[]{:S(2)}, u32[]{:S(2)}) collective-permute-start(bf16[160,256]{1,0:T(8,128)(2,1)S(1)} %get-tuple-element.311), channel_id=1, source_target_pairs={{0,1},{1,0},{2,3},{3,2},{4,5},{5,4},{6,7},{7,6},{8,9},{9,8},{10,11... | collective-permute-start | bytes 245768 | tf_op jit(solution)/shard_map/ppermute | solution.py:137
  80.4 7.3 %collective-permute-start.170 = (bf16[160,256]{1,0:T(8,128)(2,1)S(1)}, bf16[160,256]{1,0:T(8,128)(2,1)S(1)}, u32[]{:S(2)}, u32[]{:S(2)}) collective-permute-start(bf16[160,256]{1,0:T(8,128)(2,1)S(1)} %get-tuple-element.316), channel_id=1, source_target_pairs={{0,2},{2,0},{4,6},{6,4},{1,3},{3,1},{5,7},{7,5},{8,10},{10,8},{12,... | collective-permute-start | bytes 245768 | tf_op jit(solution)/shard_map/ppermute | solution.py:137
  83.4 4.4 %collective-permute-start.171 = (bf16[160,256]{1,0:T(8,128)(2,1)S(1)}, bf16[160,256]{1,0:T(8,128)(2,1)S(1)}, u32[]{:S(2)}, u32[]{:S(2)}) collective-permute-start(bf16[160,256]{1,0:T(8,128)(2,1)S(1)} %get-tuple-element.317), channel_id=1, source_target_pairs={{2,4},{4,2},{3,5},{5,3},{10,12},{12,10},{11,13},{13,11},{18,20},{2... | collective-permute-start | bytes 245768 | tf_op jit(solution)/shard_map/ppermute | solution.py:137
  84.0 4.5 %collective-permute-start.172 = (bf16[160,256]{1,0:T(8,128)(2,1)S(1)}, bf16[160,256]{1,0:T(8,128)(2,1)S(1)}, u32[]{:S(2)}, u32[]{:S(2)}) collective-permute-start(bf16[160,256]{1,0:T(8,128)(2,1)S(1)} %get-tuple-element.318), channel_id=1, source_target_pairs={{0,1},{1,0},{2,3},{3,2},{4,5},{5,4},{6,7},{7,6},{8,9},{9,8},{10,11... | collective-permute-start | bytes 245768 | tf_op jit(solution)/shard_map/ppermute | solution.py:137
where the time goes:
time: 90.3 us; the launch traced here: 90.4 us
  waiting for transfers between devices  34.7 us (38%)
  starting transfers between devices  28.2 us (31%)
  Pallas kernels  21.5 us (24%)
  between operations  2.52 us (3%)
  local copies, waits for them, and re-layouts  1.83 us (2%)
  other arithmetic  1.51 us (2%)
    pallas_call x14, Pallas kernels, call(): pl.pallas_call(kernel, out_shape=out, in_specs=[smem] * len(scalars) + [v...  21.5 us
    ppermute x12, starting transfers between devices, exchange(): lax.ppermute(rim, axis, pairs)  16.6 us
    ppermute x1, waiting for transfers between devices, model_windows(): windows[0] = lax.ppermute(windows[0], 'shot', across)  11.8 us
    ppermute x1, waiting for transfers between devices, perm(): lax.ppermute(block, 'gx', [(i, (i - by) % n_gx) for i in range(n_gx)])  8.53 us
    ppermute x2, waiting for transfers between devices, model_windows(): crossed += [lax.ppermute(send, 'shot', across) for send in sends[1:]]  8.08 us
    ppermute x12, waiting for transfers between devices, exchange(): lax.ppermute(rim, axis, pairs)  3.98 us
    ppermute x1, starting transfers between devices, model_windows(): windows[0] = lax.ppermute(windows[0], 'shot', across)  3.69 us
    ppermute x1, starting transfers between devices, model_windows(): crossed = [lax.ppermute(fields[0], 'shot', across)]  2.92 us
  transfers between devices with their start and end apart: 21, of which 9 were waited for; matrix products, arithmetic and copies ran while one was open for 4% of the time, Pallas kernels for 15%

commit v1 on v0

--- a/solution.py
+++ b/solution.py
@@ -176,7 +176,7 @@
     return jnp.dot(a, b, preferred_element_type=jnp.float32)
 
 
-def neighbours(p_ref, q_ref, dh_ref, dz_ref, high_ref, low_ref, use, before=None):
+def neighbours(p_ref, q_ref, dh_ref, dz_ref, high_ref, low_ref, use, before=None, between=None):
     nx, ny, nz = p_ref.shape
     flat = (XT * ny, nz)
     for ref in (high_ref, low_ref):
@@ -191,6 +191,8 @@
         return _
 
     lax.fori_loop(0, nx // XT, cut, None)
+    if between:
+        between()
 
     def tile(i, _):
         if before:
@@ -305,12 +307,18 @@
 
     rest = lax.rem(anchors_ref[ids_ref[0]], nx)
     first = jnp.where(rest > 0, lax.rem(rest - 1, BUCKET), 0)
+    rim_loads = [pltpu.make_async_copy(src, dst, rim_sem.at[k]) for k, (src, dst) in enumerate(zip(rims_hbm, rim_refs))]
+    for load in rim_loads:
+        load.start()
     for i in range(nx // XT):
         for load in loads(i):
             load.start()
-    rim_loads = [pltpu.make_async_copy(src, dst, rim_sem.at[k]) for k, (src, dst) in enumerate(zip(rims_hbm, rim_refs))]
-    for load in rim_loads:
-        load.start()
+    terms = []
+
+    def sums():
+        for load in rim_loads:
+            load.wait()
+        terms.extend(rim_terms(facts_ref, rim_refs, ds_ref, p_ref.shape))
 
     def arrive(i):
         for load in loads(i):
@@ -326,10 +334,7 @@
             ref[rows] = value.reshape((XT, ny, nz))
         update(0, i, rows, p, q, across, down, facts_ref, wave_ref, pb_ref, qb_ref, a, b, c, p_ref, q_ref)
 
-    neighbours(p0_ref, q0_ref, dh_ref, dz_ref, high_ref, low_ref, use, arrive)
-    for load in rim_loads:
-        load.wait()
-    terms = rim_terms(facts_ref, rim_refs, ds_ref, p_ref.shape)
+    neighbours(p0_ref, q0_ref, dh_ref, dz_ref, high_ref, low_ref, use, arrive, sums)
     add_rims(terms, p_ref, q_ref, a_ref, b_ref, p_ref, q_ref)
     put_rims_of(facts_ref, p_ref, *send_refs)
 

time: 90.3 us -> 90.7 us (level); the launches traced: 90.4 us -> 89.4 us
  waiting for transfers between devices: 34.7 us -> 32.7 us
    ppermute x1, waiting for transfers between devices: 11.8 us -> 0.01 us  [model_windows(): windows[0] = lax.ppermute(windows[0], 'shot', across)]
    ppermute x1 -> x2, waiting for transfers between devices: 8.53 us -> 17.8 us  [perm(): lax.ppermute(block, 'gx', [(i, (i - by) % n_gx) for i in range(n_gx)])]
    ppermute x1 -> x2, starting transfers between devices: 2.35 us -> 6.1 us  [perm(): lax.ppermute(block, 'gx', [(i, (i - by) % n_gx) for i in range(n_gx)])]
    ppermute x1, starting transfers between devices: 3.69 us -> 0.01 us  [model_windows(): windows[0] = lax.ppermute(windows[0], 'shot', across)]
    ppermute x2, waiting for transfers between devices: 8.08 us -> 9.84 us  [model_windows(): crossed += [lax.ppermute(send, 'shot', across) for send in sends[1:]]]
    ppermute x12, waiting for transfers between devices: 3.98 us -> 2.73 us  [exchange(): lax.ppermute(rim, axis, pairs)]
  transfers between devices with their start and end apart: 21 -> 22, of which waited for: 9 -> 8; matrix products, arithmetic and copies ran while one was open for 4% -> 4% of each run, Pallas kernels for 15% -> 15%
where the time goes in v1:
time: 90.7 us; the launch traced here: 89.4 us
  waiting for transfers between devices  32.7 us (36%)
  starting transfers between devices  29 us (32%)
  Pallas kernels  21.6 us (24%)
  between operations  2.53 us (3%)
  other arithmetic  2.37 us (3%)
  local copies, waits for them, and re-layouts  1 us (1%)
    pallas_call x14, Pallas kernels, call(): pl.pallas_call(kernel, out_shape=out, in_specs=[smem] * len(scalars) + [v...  21.6 us
    ppermute x2, waiting for transfers between devices, perm(): lax.ppermute(block, 'gx', [(i, (i - by) % n_gx) for i in range(n_gx)])  17.8 us
    ppermute x12, starting transfers between devices, exchange(): lax.ppermute(rim, axis, pairs)  17.4 us
    ppermute x2, waiting for transfers between devices, model_windows(): crossed += [lax.ppermute(send, 'shot', across) for send in sends[1:]]  9.84 us
    ppermute x2, starting transfers between devices, perm(): lax.ppermute(block, 'gx', [(i, (i - by) % n_gx) for i in range(n_gx)])  6.1 us
    ppermute x1, starting transfers between devices, model_windows(): crossed = [lax.ppermute(fields[0], 'shot', across)]  2.92 us
    ppermute x12, waiting for transfers between devices, exchange(): lax.ppermute(rim, axis, pairs)  2.73 us
    ppermute x1, waiting for transfers between devices, model_windows(): crossed = [lax.ppermute(fields[0], 'shot', across)]  2.25 us
  transfers between devices with their start and end apart: 22, of which 8 were waited for; matrix products, arithmetic and copies ran while one was open for 4% of the time, Pallas kernels for 15%

profile of v1, /device:TPU:0, one launch (start us, length us, event | category | flops | bytes accessed | tf_op | source)
XLA Modules:
  0.0 89.4 jit_solution(7559184540853923056)
XLA Ops:
  0.6 0.5 collective-permute-start.153
  1.1 0.1 collective-permute-start.154
  1.2 2.9 %collective-permute-start.155 = (bf16[32,32,256]{2,1,0:T(8,128)(2,1)}, bf16[32,32,256]{2,1,0:T(8,128)(2,1)S(1)}, u32[]{:S(2)}, u32[]{:S(2)}) collective-permute-start(bf16[32,32,256]{2,1,0:T(8,128)(2,1)} %refs_0_.1), channel_id=1, source_target_pairs={{0,16},{8,24},{16,0},{24,8},{1,17},{9,25},{17,1},{25,9},{2,18},{10... | collective-permute-start | bytes 1572872 | tf_op jit(solution)/shard_map/ppermute | solution.py:108
  4.1 0.7 pad_add_fusion.ids_ref
  4.8 1.2 %facts.1 = (s32[8,256]{1,0:T(8,128)S(1)}, f32[4,256]{1,0:T(4,128)S(1)}, s32[1]{0:T(128)}, s32[1]{0:T(128)}) custom-call(s32[3]{0:T(128)} %pad_add_fusion.ids_ref, s32[4]{0:T(128)} %anchors_ref.13, s32[1,3]{1,0:T(1,128)} %sources_ref.1, f32[1,4]{1,0:T(1,128)} %wavelet_ref.1), custom_call_target="tpu_custom_call" | custom-call | tf_op jit(solution)/shard_map/facts/pallas_call | solution.py:391
  6.0 0.0 copy-start.6
  6.0 1.4 %edges.1 = (bf16[160,256]{1,0:T(8,128)(2,1)S(1)}, bf16[160,256]{1,0:T(8,128)(2,1)S(1)}, bf16[160,256]{1,0:T(8,128)(2,1)S(1)}) custom-call(s32[8,256]{1,0:T(8,128)S(1)} %get-tuple-element.271.facts_ref, f32[32,32,256]{2,1,0:T(8,128)} %bitcast.11), custom_call_target="tpu_custom_call" | custom-call | tf_op jit(solution)/shard_map/edges/pallas_call | solution.py:391
  7.4 1.6 %collective-permute-start.156 = (bf16[160,256]{1,0:T(8,128)(2,1)S(1)}, bf16[160,256]{1,0:T(8,128)(2,1)S(1)}, u32[]{:S(2)}, u32[]{:S(2)}) collective-permute-start(bf16[160,256]{1,0:T(8,128)(2,1)S(1)} %get-tuple-element.275), channel_id=1, source_target_pairs={{0,2},{2,0},{4,6},{6,4},{1,3},{3,1},{5,7},{7,5},{8,10},{10,8},{12,... | collective-permute-start | bytes 245768 | tf_op jit(solution)/shard_map/ppermute | solution.py:137
  9.1 0.7 collective-permute-start.157
  9.7 0.0 copy-start.5
  9.7 0.0 copy-start.7
  9.8 1.6 %collective-permute-start.158 = (bf16[160,256]{1,0:T(8,128)(2,1)S(1)}, bf16[160,256]{1,0:T(8,128)(2,1)S(1)}, u32[]{:S(2)}, u32[]{:S(2)}) collective-permute-start(bf16[160,256]{1,0:T(8,128)(2,1)S(1)} %get-tuple-element.277), channel_id=1, source_target_pairs={{0,1},{1,0},{2,3},{3,2},{4,5},{5,4},{6,7},{7,6},{8,9},{9,8},{10,11... | collective-permute-start | bytes 245768 | tf_op jit(solution)/shard_map/ppermute | solution.py:137
  11.3 1.6 %pick_1.1 = (bf16[32,32,256]{2,1,0:T(8,128)(2,1)}, bf16[32,32,256]{2,1,0:T(8,128)(2,1)S(1)}) custom-call(s32[3]{0:T(128)} %pad_add_fusion.ids_ref, s32[4]{0:T(128)} %anchors_ref.13, bf16[32,32,256]{2,1,0:T(8,128)(2,1)S(1)} %copy-done.6, bf16[32,32,256]{2,1,0:T(8,128)(2,1)S(1)} %collective-permute-done.153.other_ref), custom_call_target="tpu_custom_call" | custom-call | tf_op jit(solution)/shard_map/pick_1/pallas_call | solution.py:391
  12.9 0.0 collective-permute-done.154.other_ref
  13.0 0.8 pick_2.1
  13.8 0.0 collective-permute-done.156.refs_5_
  13.8 0.0 collective-permute-done.157.refs_6_
  13.8 0.4 collective-permute-done.158.refs_7_
  14.3 2.3 %collective-permute-done.155.refs_1_ = bf16[32,32,256]{2,1,0:T(8,128)(2,1)S(1)} collective-permute-done((bf16[32,32,256]{2,1,0:T(8,128)(2,1)}, bf16[32,32,256]{2,1,0:T(8,128)(2,1)S(1)}, u32[]{:S(2)}, u32[]{:S(2)}) %collective-permute-start.155) | collective-permute-done | bytes 524320 | tf_op jit(solution)/shard_map/ppermute | solution.py:108
  16.5 0.0 collective-permute-start.162
  16.5 1.7 %collective-permute-start.160 = (bf16[32,32,256]{2,1,0:T(8,128)(2,1)}, bf16[32,32,256]{2,1,0:T(8,128)(2,1)S(1)}, u32[]{:S(2)}, u32[]{:S(2)}) collective-permute-start(bf16[32,32,256]{2,1,0:T(8,128)(2,1)} %get-tuple-element.281), channel_id=1, source_target_pairs={{0,16},{8,24},{16,0},{24,8},{1,17},{9,25},{17,1},{25,9},{2,18},{10... | collective-permute-start | bytes 1572872 | tf_op jit(solution)/shard_map/ppermute | solution.py:118
  18.3 0.3 collective-permute-start.159
  19.9 0.0 collective-permute-done.161.refs_2_
  19.9 0.8 join_0.1
  20.7 0.9 conditional.3
  20.8 0.9 concatenate.216
  21.6 9.8 %collective-permute-done.160.refs_1_ = bf16[32,32,256]{2,1,0:T(8,128)(2,1)S(1)} collective-permute-done((bf16[32,32,256]{2,1,0:T(8,128)(2,1)}, bf16[32,32,256]{2,1,0:T(8,128)(2,1)S(1)}, u32[]{:S(2)}, u32[]{:S(2)}) %collective-permute-start.160) | collective-permute-done | bytes 524320 | tf_op jit(solution)/shard_map/ppermute | solution.py:118
  31.5 0.7 join_1.1
  32.2 13.8 %conditional.4 = (bf16[35,32,256]{2,1,0:T(8,128)(2,1)}) conditional(s32[]{:T(128)} %bitcast.8, bf16[32,32,256]{2,1,0:T(8,128)(2,1)S(1)} %join_1.1, bf16[32,32,256]{2,1,0:T(8,128)(2,1)S(1)} %join_1.1, bf16[32,32,256]{2,1,0:T(8,128)(2,1)S(1)} %join_1.1, bf16[32,32,256]{2,1,0:T(8,128)(2,1)S(1)} %join_1.1, ...), branch_computations={%region_36.0_spmd, %region_37.0_spmd, %region_38.0_spmd, %region_3... | conditional | flops 286720 | bytes 4587608 | solution.py:106
  32.3 3.9 %collective-permute-start.63 = (bf16[28,32,256]{2,1,0:T(8,128)(2,1)S(1)}, bf16[28,32,256]{2,1,0:T(8,128)(2,1)S(1)}, u32[]{:S(2)}, u32[]{:S(2)}) collective-permute-start(bf16[28,32,256]{2,1,0:T(8,128)(2,1)S(1)} %slice.433), channel_id=1, source_target_pairs={{0,6},{2,0},{4,2},{6,4},{1,7},{3,1},{5,3},{7,5},{8,14},{10,8},{12,... | collective-permute-start | bytes 1376264 | tf_op jit(solution)/shard_map/cond/branch_7_fun/ppermute | solution.py:76
  36.2 9.0 %collective-permute-done.63 = bf16[28,32,256]{2,1,0:T(8,128)(2,1)S(1)} collective-permute-done((bf16[28,32,256]{2,1,0:T(8,128)(2,1)S(1)}, bf16[28,32,256]{2,1,0:T(8,128)(2,1)S(1)}, u32[]{:S(2)}, u32[]{:S(2)}) %collective-permute-start.63) | collective-permute-done | bytes 458784 | tf_op jit(solution)/shard_map/cond/branch_7_fun/ppermute | solution.py:76
  45.2 0.9 pad_maximum_fusion.38
  46.0 0.7 join_2.1
  46.8 0.0 copy-start
  46.8 0.0 copy-start.1
  46.8 0.0 copy-start.2
  46.8 0.0 copy-start.3
  46.9 0.0 copy-start.4
  46.9 12.1 %conditional.5 = (bf16[35,32,256]{2,1,0:T(8,128)(2,1)}) conditional(s32[]{:T(128)} %bitcast.8, bf16[32,32,256]{2,1,0:T(8,128)(2,1)S(1)} %join_2.1, bf16[32,32,256]{2,1,0:T(8,128)(2,1)S(1)} %join_2.1, bf16[32,32,256]{2,1,0:T(8,128)(2,1)S(1)} %join_2.1, bf16[32,32,256]{2,1,0:T(8,128)(2,1)S(1)} %join_2.1, ...), branch_computations={%region_72.0_spmd, %region_73.0_spmd, %region_74.0_spmd, %region_7... | conditional | flops 286720 | bytes 4587608 | solution.py:106
  47.0 2.2 %collective-permute-start.111 = (bf16[28,32,256]{2,1,0:T(8,128)(2,1)S(1)}, bf16[28,32,256]{2,1,0:T(8,128)(2,1)S(1)}, u32[]{:S(2)}, u32[]{:S(2)}) collective-permute-start(bf16[28,32,256]{2,1,0:T(8,128)(2,1)S(1)} %slice.493), channel_id=1, source_target_pairs={{0,6},{2,0},{4,2},{6,4},{1,7},{3,1},{5,3},{7,5},{8,14},{10,8},{12,... | collective-permute-start | bytes 1376264 | tf_op jit(solution)/shard_map/cond/branch_7_fun/ppermute | solution.py:76
  49.2 8.9 %collective-permute-done.111 = bf16[28,32,256]{2,1,0:T(8,128)(2,1)S(1)} collective-permute-done((bf16[28,32,256]{2,1,0:T(8,128)(2,1)S(1)}, bf16[28,32,256]{2,1,0:T(8,128)(2,1)S(1)}, u32[]{:S(2)}, u32[]{:S(2)}) %collective-permute-start.111) | collective-permute-done | bytes 458784 | tf_op jit(solution)/shard_map/cond/branch_7_fun/ppermute | solution.py:76
  58.1 0.9 pad_maximum_fusion.70
  58.9 0.0 collective-permute-done.163.refs_2_
  59.0 5.2 %first.1 = (f32[32,32,256]{2,1,0:T(8,128)S(1)}, f32[32,32,256]{2,1,0:T(8,128)S(1)}, f32[32,32,256]{2,1,0:T(8,128)S(1)}, f32[32,32,256]{2,1,0:T(8,128)S(1)}, f32[...) custom-call(s32[3]{0:T(128)} %pad_add_fusion.ids_ref, ...), custom_call_target="tpu_custom_call" | custom-call | tf_op jit(solution)/shard_map/first/pallas_call | solution.py:391
  64.1 0.6 collective-permute-start.164
  64.8 0.7 collective-permute-start.165
  65.4 1.6 %collective-permute-start.166 = (bf16[160,256]{1,0:T(8,128)(2,1)S(1)}, bf16[160,256]{1,0:T(8,128)(2,1)S(1)}, u32[]{:S(2)}, u32[]{:S(2)}) collective-permute-start(bf16[160,256]{1,0:T(8,128)(2,1)S(1)} %get-tuple-element.304), channel_id=1, source_target_pairs={{0,1},{1,0},{2,3},{3,2},{4,5},{5,4},{6,7},{7,6},{8,9},{9,8},{10,11... | collective-permute-start | bytes 245768 | tf_op jit(solution)/shard_map/ppermute | solution.py:137
  67.0 2.1 %inner_1.1 = (f32[32,32,256]{2,1,0:T(8,128)S(1)}, f32[32,32,256]{2,1,0:T(8,128)S(1)}) custom-call(s32[8,256]{1,0:T(8,128)S(1)} %get-tuple-element.271.facts_ref, f32[4,256]{1,0:T(4,128)S(1)} %get-tuple-element.272.wave_ref, f32[32,32,256]{2,1,0:T(8,128)S(1)} %get-tuple-element.295.p_ref.pb_ref, f32[32,32,256]{2,1,0:T(8,128)S(1)} %bitcast.13, ...), custom_call_target="tpu_custom_call" | custom-call | tf_op jit(solution)/shard_map/inner_1/pallas_call | solution.py:391
  69.2 0.0 collective-permute-done.164.refs_0_
  69.2 0.0 collective-permute-done.165.refs_1_
  69.2 0.7 collective-permute-done.166.refs_2_
  69.9 0.6 rims_1.1
  70.5 3.9 %collective-permute-start.167 = (bf16[160,256]{1,0:T(8,128)(2,1)S(1)}, bf16[160,256]{1,0:T(8,128)(2,1)S(1)}, u32[]{:S(2)}, u32[]{:S(2)}) collective-permute-start(bf16[160,256]{1,0:T(8,128)(2,1)S(1)} %get-tuple-element.309), channel_id=1, source_target_pairs={{0,2},{2,0},{4,6},{6,4},{1,3},{3,1},{5,7},{7,5},{8,10},{10,8},{12,... | collective-permute-start | bytes 245768 | tf_op jit(solution)/shard_map/ppermute | solution.py:137
  74.4 0.7 collective-permute-start.168
  75.1 1.6 %collective-permute-start.169 = (bf16[160,256]{1,0:T(8,128)(2,1)S(1)}, bf16[160,256]{1,0:T(8,128)(2,1)S(1)}, u32[]{:S(2)}, u32[]{:S(2)}) collective-permute-start(bf16[160,256]{1,0:T(8,128)(2,1)S(1)} %get-tuple-element.311), channel_id=1, source_target_pairs={{0,1},{1,0},{2,3},{3,2},{4,5},{5,4},{6,7},{7,6},{8,9},{9,8},{10,11... | collective-permute-start | bytes 245768 | tf_op jit(solution)/shard_map/ppermute | solution.py:137
  76.7 2.1 %inner_2.1 = (f32[32,32,256]{2,1,0:T(8,128)S(1)}, f32[32,32,256]{2,1,0:T(8,128)S(1)}) custom-call(s32[8,256]{1,0:T(8,128)S(1)} %get-tuple-element.271.facts_ref, f32[4,256]{1,0:T(4,128)S(1)} %get-tuple-element.272.wave_ref, f32[32,32,256]{2,1,0:T(8,128)S(1)} %get-tuple-element.305.p_ref.pb_ref, f32[32,32,256]{2,1,0:T(8,128)S(1)} %get-tuple-element.295.p_ref.pb_ref, ...), custom_call_target="tpu_custom_call" | custom-call | tf_op jit(solution)/shard_map/inner_2/pallas_call | solution.py:391
  78.8 0.8 collective-permute-done.169.refs_2_
  79.6 0.6 rims_2.1
  80.2 2.2 %collective-permute-start.170 = (bf16[160,256]{1,0:T(8,128)(2,1)S(1)}, bf16[160,256]{1,0:T(8,128)(2,1)S(1)}, u32[]{:S(2)}, u32[]{:S(2)}) collective-permute-start(bf16[160,256]{1,0:T(8,128)(2,1)S(1)} %get-tuple-element.316), channel_id=1, source_target_pairs={{0,2},{2,0},{4,6},{6,4},{1,3},{3,1},{5,7},{7,5},{8,10},{10,8},{12,... | collective-permute-start | bytes 245768 | tf_op jit(solution)/shard_map/ppermute | solution.py:137
  82.4 0.7 collective-permute-start.171
  83.1 1.6 %collective-permute-start.172 = (bf16[160,256]{1,0:T(8,128)(2,1)S(1)}, bf16[160,256]{1,0:T(8,128)(2,1)S(1)}, u32[]{:S(2)}, u32[]{:S(2)}) collective-permute-start(bf16[160,256]{1,0:T(8,128)(2,1)S(1)} %get-tuple-element.318), channel_id=1, source_target_pairs={{0,1},{1,0},{2,3},{3,2},{4,5},{5,4},{6,7},{7,6},{8,9},{9,8},{10,11... | collective-permute-start | bytes 245768 | tf_op jit(solution)/shard_map/ppermute | solution.py:137
  84.7 2.1 %inner_3.1 = (f32[32,32,256]{2,1,0:T(8,128)S(1)}, f32[32,32,256]{2,1,0:T(8,128)S(1)}) custom-call(s32[8,256]{1,0:T(8,128)S(1)} %get-tuple-element.271.facts_ref, f32[4,256]{1,0:T(4,128)S(1)} %get-tuple-element.272.wave_ref, f32[32,32,256]{2,1,0:T(8,128)S(1)} %get-tuple-element.312.p_ref, f32[32,32,256]{2,1,0:T(8,128)S(1)} %get-tuple-element.305.p_ref.pb_ref, ...), custom_call_target="tpu_custom_call" | custom-call | tf_op jit(solution)/shard_map/inner_3/pallas_call | solution.py:391
  86.8 0.8 collective-permute-done.172.refs_2_
  87.6 1.7 %rims_3.1 = (f32[32,32,256]{2,1,0:T(8,128)S(1)}, f32[32,32,256]{2,1,0:T(8,128)S(1)}, f32[32,32,256]{2,1,0:T(8,128)}, f32[32,32,256]{2,1,0:T(8,128)}) custom-call(s32[8,256]{1,0:T(8,128)S(1)} %get-tuple-element.271.facts_ref, f32[32,32,256]{2,1,0:T(8,128)S(1)} %get-tuple-element.314.p_in, ...), custom_call_target="tpu_custom_call", output_to_operand_aliasing={{0}: (1, {}), {1}: (2, {})} | custom-call | tf_op jit(solution)/shard_map/rims_3/pallas_call | solution.py:391
  (27 shorter events, 0.1 us)
Async XLA Ops:
  0.6 9.1 %collective-permute-start.153 = (bf16[32,32,256]{2,1,0:T(8,128)(2,1)}, bf16[32,32,256]{2,1,0:T(8,128)(2,1)S(1)}, u32[]{:S(2)}, u32[]{:S(2)}) collective-permute-start(bf16[32,32,256]{2,1,0:T(8,128)(2,1)} %field_ref.2), channel_id=1, source_target_pairs={{0,8},{8,0},{16,24},{24,16},{1,9},{9,1},{17,25},{25,17},{2,10},{10... | collective-permute-start | bytes 1572872 | tf_op jit(solution)/shard_map/ppermute | solution.py:109
  1.1 11.8 %collective-permute-start.154 = (bf16[32,32,256]{2,1,0:T(8,128)(2,1)}, bf16[32,32,256]{2,1,0:T(8,128)(2,1)S(1)}, u32[]{:S(2)}, u32[]{:S(2)}) collective-permute-start(bf16[32,32,256]{2,1,0:T(8,128)(2,1)} %field_ref.3), channel_id=1, source_target_pairs={{0,8},{8,0},{16,24},{24,16},{1,9},{9,1},{17,25},{25,17},{2,10},{10... | collective-permute-start | bytes 1572872 | tf_op jit(solution)/shard_map/ppermute | solution.py:109
  1.2 15.3 %collective-permute-start.155 = (bf16[32,32,256]{2,1,0:T(8,128)(2,1)}, bf16[32,32,256]{2,1,0:T(8,128)(2,1)S(1)}, u32[]{:S(2)}, u32[]{:S(2)}) collective-permute-start(bf16[32,32,256]{2,1,0:T(8,128)(2,1)} %refs_0_.1), channel_id=1, source_target_pairs={{0,16},{8,24},{16,0},{24,8},{1,17},{9,25},{17,1},{25,9},{2,18},{10... | collective-permute-start | bytes 1572872 | tf_op jit(solution)/shard_map/ppermute | solution.py:108
  6.0 5.3 %copy-start.6 = (bf16[32,32,256]{2,1,0:T(8,128)(2,1)S(1)}, bf16[32,32,256]{2,1,0:T(8,128)(2,1)}, u32[]{:S(2)}) copy-start(bf16[32,32,256]{2,1,0:T(8,128)(2,1)} %field_ref.2) | copy-start | bytes 1572868
  7.4 6.4 %collective-permute-start.156 = (bf16[160,256]{1,0:T(8,128)(2,1)S(1)}, bf16[160,256]{1,0:T(8,128)(2,1)S(1)}, u32[]{:S(2)}, u32[]{:S(2)}) collective-permute-start(bf16[160,256]{1,0:T(8,128)(2,1)S(1)} %get-tuple-element.275), channel_id=1, source_target_pairs={{0,2},{2,0},{4,6},{6,4},{1,3},{3,1},{5,7},{7,5},{8,10},{10,8},{12,... | collective-permute-start | bytes 245768 | tf_op jit(solution)/shard_map/ppermute | solution.py:137
  9.1 4.7 %collective-permute-start.157 = (bf16[160,256]{1,0:T(8,128)(2,1)S(1)}, bf16[160,256]{1,0:T(8,128)(2,1)S(1)}, u32[]{:S(2)}, u32[]{:S(2)}) collective-permute-start(bf16[160,256]{1,0:T(8,128)(2,1)S(1)} %get-tuple-element.276), channel_id=1, source_target_pairs={{2,4},{4,2},{3,5},{5,3},{10,12},{12,10},{11,13},{13,11},{18,20},{2... | collective-permute-start | bytes 245768 | tf_op jit(solution)/shard_map/ppermute | solution.py:137
  9.7 3.2 %copy-start.5 = (bf16[32,32,256]{2,1,0:T(8,128)(2,1)S(1)}, bf16[32,32,256]{2,1,0:T(8,128)(2,1)}, u32[]{:S(2)}) copy-start(bf16[32,32,256]{2,1,0:T(8,128)(2,1)} %refs_0_.1) | copy-start | bytes 1572868
  9.7 3.2 %copy-start.7 = (bf16[32,32,256]{2,1,0:T(8,128)(2,1)S(1)}, bf16[32,32,256]{2,1,0:T(8,128)(2,1)}, u32[]{:S(2)}) copy-start(bf16[32,32,256]{2,1,0:T(8,128)(2,1)} %field_ref.3) | copy-start | bytes 1572868
  9.8 4.5 %collective-permute-start.158 = (bf16[160,256]{1,0:T(8,128)(2,1)S(1)}, bf16[160,256]{1,0:T(8,128)(2,1)S(1)}, u32[]{:S(2)}, u32[]{:S(2)}) collective-permute-start(bf16[160,256]{1,0:T(8,128)(2,1)S(1)} %get-tuple-element.277), channel_id=1, source_target_pairs={{0,1},{1,0},{2,3},{3,2},{4,5},{5,4},{6,7},{7,6},{8,9},{9,8},{10,11... | collective-permute-start | bytes 245768 | tf_op jit(solution)/shard_map/ppermute | solution.py:137
  12.9 6.9 %collective-permute-start.161 = (bf16[32,32,256]{2,1,0:T(8,128)(2,1)S(1)}, bf16[32,32,256]{2,1,0:T(8,128)(2,1)S(1)}, u32[]{:S(2)}, u32[]{:S(2)}) collective-permute-start(bf16[32,32,256]{2,1,0:T(8,128)(2,1)S(1)} %copy-done.5), channel_id=1, source_target_pairs={{0,8},{8,0},{16,24},{24,16},{1,9},{9,1},{17,25},{25,17},{2,10},{10... | collective-permute-start | bytes 1572872 | tf_op jit(solution)/shard_map/ppermute | solution.py:109
  13.8 6.9 %copy-start.8 = (bf16[160,256]{1,0:T(8,128)(2,1)}, bf16[160,256]{1,0:T(8,128)(2,1)S(1)}, u32[]{:S(2)}) copy-start(bf16[160,256]{1,0:T(8,128)(2,1)S(1)} %collective-permute-done.156.refs_5_) | copy-start | bytes 245764
  13.8 6.1 %copy-start.9 = (bf16[160,256]{1,0:T(8,128)(2,1)}, bf16[160,256]{1,0:T(8,128)(2,1)S(1)}, u32[]{:S(2)}) copy-start(bf16[160,256]{1,0:T(8,128)(2,1)S(1)} %collective-permute-done.157.refs_6_) | copy-start | bytes 245764
  14.3 5.6 %copy-start.10 = (bf16[160,256]{1,0:T(8,128)(2,1)}, bf16[160,256]{1,0:T(8,128)(2,1)S(1)}, u32[]{:S(2)}) copy-start(bf16[160,256]{1,0:T(8,128)(2,1)S(1)} %collective-permute-done.158.refs_7_) | copy-start | bytes 245764
  16.5 3.4 %collective-permute-start.162 = (bf16[32,32,256]{2,1,0:T(8,128)(2,1)S(1)}, bf16[32,32,256]{2,1,0:T(8,128)(2,1)S(1)}, u32[]{:S(2)}, u32[]{:S(2)}) collective-permute-start(bf16[32,32,256]{2,1,0:T(8,128)(2,1)S(1)} %collective-permute-done.155.refs_1_), channel_id=1, source_target_pairs={{0,8},{8,0},{16,24},{24,16},{1,9},{9,1},{17,25},{25,17},{2,10},{10... | collective-permute-start | bytes 1572872 | tf_op jit(solution)/shard_map/ppermute | solution.py:119
  16.5 14.9 %collective-permute-start.160 = (bf16[32,32,256]{2,1,0:T(8,128)(2,1)}, bf16[32,32,256]{2,1,0:T(8,128)(2,1)S(1)}, u32[]{:S(2)}, u32[]{:S(2)}) collective-permute-start(bf16[32,32,256]{2,1,0:T(8,128)(2,1)} %get-tuple-element.281), channel_id=1, source_target_pairs={{0,16},{8,24},{16,0},{24,8},{1,17},{9,25},{17,1},{25,9},{2,18},{10... | collective-permute-start | bytes 1572872 | tf_op jit(solution)/shard_map/ppermute | solution.py:118
  18.3 27.8 %collective-permute-start.159 = (bf16[32,32,256]{2,1,0:T(8,128)(2,1)S(1)}, bf16[32,32,256]{2,1,0:T(8,128)(2,1)S(1)}, u32[]{:S(2)}, u32[]{:S(2)}) collective-permute-start(bf16[32,32,256]{2,1,0:T(8,128)(2,1)S(1)} %get-tuple-element.280), channel_id=1, source_target_pairs={{0,16},{8,24},{16,0},{24,8},{1,17},{9,25},{17,1},{25,9},{2,18},{10... | collective-permute-start | bytes 1572872 | tf_op jit(solution)/shard_map/ppermute | solution.py:118
  32.3 12.9 %collective-permute-start.63 = (bf16[28,32,256]{2,1,0:T(8,128)(2,1)S(1)}, bf16[28,32,256]{2,1,0:T(8,128)(2,1)S(1)}, u32[]{:S(2)}, u32[]{:S(2)}) collective-permute-start(bf16[28,32,256]{2,1,0:T(8,128)(2,1)S(1)} %slice.433), channel_id=1, source_target_pairs={{0,6},{2,0},{4,2},{6,4},{1,7},{3,1},{5,3},{7,5},{8,14},{10,8},{12,... | collective-permute-start | bytes 1376264 | tf_op jit(solution)/shard_map/cond/branch_7_fun/ppermute | solution.py:76
  46.0 12.9 %collective-permute-start.163 = (bf16[35,32,256]{2,1,0:T(8,128)(2,1)}, bf16[35,32,256]{2,1,0:T(8,128)(2,1)S(1)}, u32[]{:S(2)}, u32[]{:S(2)}) collective-permute-start(bf16[35,32,256]{2,1,0:T(8,128)(2,1)} %get-tuple-element.321), channel_id=1, source_target_pairs={{0,16},{8,24},{16,0},{24,8},{1,17},{9,25},{17,1},{25,9},{2,18},{10... | collective-permute-start | bytes 1720328 | tf_op jit(solution)/shard_map/ppermute | solution.py:124
  46.8 12.1 %copy-start = (f32[1,32,32,256]{3,2,1,0:T(8,128)S(1)}, f32[1,32,32,256]{3,2,1,0:T(8,128)}, u32[]{:S(2)}) copy-start(f32[1,32,32,256]{3,2,1,0:T(8,128)} %param.127) | copy-start | bytes 3145732
  46.8 12.1 %copy-start.1 = (bf16[512,320]{1,0:T(8,128)(2,1)S(1)}, bf16[512,320]{1,0:T(8,128)(2,1)}, u32[]{:S(2)}) copy-start(bf16[512,320]{1,0:T(8,128)(2,1)} %constant.51.clone.ds_ref.refs_3_) | copy-start | bytes 983044
  46.8 12.1 %copy-start.2 = (bf16[256,512]{1,0:T(8,128)(2,1)S(1)}, bf16[256,512]{1,0:T(8,128)(2,1)}, u32[]{:S(2)}) copy-start(bf16[256,512]{1,0:T(8,128)(2,1)} %constant.50.clone.dh_ref) | copy-start | bytes 786436
  46.8 12.1 %copy-start.3 = (f32[1,32,32,256]{3,2,1,0:T(8,128)S(1)}, f32[1,32,32,256]{3,2,1,0:T(8,128)}, u32[]{:S(2)}) copy-start(f32[1,32,32,256]{3,2,1,0:T(8,128)} %param.129) | copy-start | bytes 3145732
  46.9 12.1 %copy-start.4 = (bf16[256,256]{1,0:T(8,128)(2,1)S(1)}, bf16[256,256]{1,0:T(8,128)(2,1)}, u32[]{:S(2)}) copy-start(bf16[256,256]{1,0:T(8,128)(2,1)} %constant.49.clone.dz_ref) | copy-start | bytes 393220
  47.0 11.1 %collective-permute-start.111 = (bf16[28,32,256]{2,1,0:T(8,128)(2,1)S(1)}, bf16[28,32,256]{2,1,0:T(8,128)(2,1)S(1)}, u32[]{:S(2)}, u32[]{:S(2)}) collective-permute-start(bf16[28,32,256]{2,1,0:T(8,128)(2,1)S(1)} %slice.493), channel_id=1, source_target_pairs={{0,6},{2,0},{4,2},{6,4},{1,7},{3,1},{5,3},{7,5},{8,14},{10,8},{12,... | collective-permute-start | bytes 1376264 | tf_op jit(solution)/shard_map/cond/branch_7_fun/ppermute | solution.py:76
  64.1 5.0 %collective-permute-start.164 = (bf16[160,256]{1,0:T(8,128)(2,1)S(1)}, bf16[160,256]{1,0:T(8,128)(2,1)S(1)}, u32[]{:S(2)}, u32[]{:S(2)}) collective-permute-start(bf16[160,256]{1,0:T(8,128)(2,1)S(1)} %get-tuple-element.302), channel_id=1, source_target_pairs={{0,2},{2,0},{4,6},{6,4},{1,3},{3,1},{5,7},{7,5},{8,10},{10,8},{12,... | collective-permute-start | bytes 245768 | tf_op jit(solution)/shard_map/ppermute | solution.py:137
  64.8 4.4 %collective-permute-start.165 = (bf16[160,256]{1,0:T(8,128)(2,1)S(1)}, bf16[160,256]{1,0:T(8,128)(2,1)S(1)}, u32[]{:S(2)}, u32[]{:S(2)}) collective-permute-start(bf16[160,256]{1,0:T(8,128)(2,1)S(1)} %get-tuple-element.303), channel_id=1, source_target_pairs={{2,4},{4,2},{3,5},{5,3},{10,12},{12,10},{11,13},{13,11},{18,20},{2... | collective-permute-start | bytes 245768 | tf_op jit(solution)/shard_map/ppermute | solution.py:137
  65.4 4.5 %collective-permute-start.166 = (bf16[160,256]{1,0:T(8,128)(2,1)S(1)}, bf16[160,256]{1,0:T(8,128)(2,1)S(1)}, u32[]{:S(2)}, u32[]{:S(2)}) collective-permute-start(bf16[160,256]{1,0:T(8,128)(2,1)S(1)} %get-tuple-element.304), channel_id=1, source_target_pairs={{0,1},{1,0},{2,3},{3,2},{4,5},{5,4},{6,7},{7,6},{8,9},{9,8},{10,11... | collective-permute-start | bytes 245768 | tf_op jit(solution)/shard_map/ppermute | solution.py:137
  70.5 8.3 %collective-permute-start.167 = (bf16[160,256]{1,0:T(8,128)(2,1)S(1)}, bf16[160,256]{1,0:T(8,128)(2,1)S(1)}, u32[]{:S(2)}, u32[]{:S(2)}) collective-permute-start(bf16[160,256]{1,0:T(8,128)(2,1)S(1)} %get-tuple-element.309), channel_id=1, source_target_pairs={{0,2},{2,0},{4,6},{6,4},{1,3},{3,1},{5,7},{7,5},{8,10},{10,8},{12,... | collective-permute-start | bytes 245768 | tf_op jit(solution)/shard_map/ppermute | solution.py:137
  74.4 4.4 %collective-permute-start.168 = (bf16[160,256]{1,0:T(8,128)(2,1)S(1)}, bf16[160,256]{1,0:T(8,128)(2,1)S(1)}, u32[]{:S(2)}, u32[]{:S(2)}) collective-permute-start(bf16[160,256]{1,0:T(8,128)(2,1)S(1)} %get-tuple-element.310), channel_id=1, source_target_pairs={{2,4},{4,2},{3,5},{5,3},{10,12},{12,10},{11,13},{13,11},{18,20},{2... | collective-permute-start | bytes 245768 | tf_op jit(solution)/shard_map/ppermute | solution.py:137
  75.1 4.5 %collective-permute-start.169 = (bf16[160,256]{1,0:T(8,128)(2,1)S(1)}, bf16[160,256]{1,0:T(8,128)(2,1)S(1)}, u32[]{:S(2)}, u32[]{:S(2)}) collective-permute-start(bf16[160,256]{1,0:T(8,128)(2,1)S(1)} %get-tuple-element.311), channel_id=1, source_target_pairs={{0,1},{1,0},{2,3},{3,2},{4,5},{5,4},{6,7},{7,6},{8,9},{9,8},{10,11... | collective-permute-start | bytes 245768 | tf_op jit(solution)/shard_map/ppermute | solution.py:137
  80.2 6.6 %collective-permute-start.170 = (bf16[160,256]{1,0:T(8,128)(2,1)S(1)}, bf16[160,256]{1,0:T(8,128)(2,1)S(1)}, u32[]{:S(2)}, u32[]{:S(2)}) collective-permute-start(bf16[160,256]{1,0:T(8,128)(2,1)S(1)} %get-tuple-element.316), channel_id=1, source_target_pairs={{0,2},{2,0},{4,6},{6,4},{1,3},{3,1},{5,7},{7,5},{8,10},{10,8},{12,... | collective-permute-start | bytes 245768 | tf_op jit(solution)/shard_map/ppermute | solution.py:137
  82.4 4.4 %collective-permute-start.171 = (bf16[160,256]{1,0:T(8,128)(2,1)S(1)}, bf16[160,256]{1,0:T(8,128)(2,1)S(1)}, u32[]{:S(2)}, u32[]{:S(2)}) collective-permute-start(bf16[160,256]{1,0:T(8,128)(2,1)S(1)} %get-tuple-element.317), channel_id=1, source_target_pairs={{2,4},{4,2},{3,5},{5,3},{10,12},{12,10},{11,13},{13,11},{18,20},{2... | collective-permute-start | bytes 245768 | tf_op jit(solution)/shard_map/ppermute | solution.py:137
  83.1 4.5 %collective-permute-start.172 = (bf16[160,256]{1,0:T(8,128)(2,1)S(1)}, bf16[160,256]{1,0:T(8,128)(2,1)S(1)}, u32[]{:S(2)}, u32[]{:S(2)}) collective-permute-start(bf16[160,256]{1,0:T(8,128)(2,1)S(1)} %get-tuple-element.318), channel_id=1, source_target_pairs={{0,1},{1,0},{2,3},{3,2},{4,5},{5,4},{6,7},{7,6},{8,9},{9,8},{10,11... | collective-permute-start | bytes 245768 | tf_op jit(solution)/shard_map/ppermute | solution.py:137
